TPU v7x, 128 devices: a whole 4x4x4 slice. The times are simulated.
128 devices in a mesh: outer: 16 (over x_lo, y, core), inner: 8 (over x_hi, z).
Axes of the slice: x: 4 (x_hi: 2, x_lo: 2; x = x_hi * 2 + x_lo), y: 4, z: 4, core: 2. Of those that a mesh axis runs over, the one named last changes fastest.
Arguments:
- queries: bfloat16 [16384, 6144], P(('outer', 'inner')), may hold values from -8 to 8
- compressed: bfloat16 [16384, 576], P(('outer', 'inner')), may hold values from -8 to 8
- kv_weight: bfloat16 [512, 8192], replicated, may hold values from -0.25 to 0.25
- segments: int32 [128], replicated, may hold values from 0 to 31, never falling along the last dimension, each value on 1 to 8 neighbouring positions
- grad_out: bfloat16 [16384, 4096], P(('outer', 'inner')), may hold values from -6 to 6
Outputs:
- attended: bfloat16 [16384, 4096], P(('outer', 'inner'))
- grad_queries: bfloat16 [16384, 6144], P(('outer', 'inner'))
- grad_compressed: bfloat16 [16384, 576], P(('outer', 'inner'))
- grad_weight_t: float32 [8192, 512], P(('outer', 'inner'))
Inputs may be any that keep to these rules, and one draw needn't show every extreme that they name: `segments`: ids never fall along the sequence; every document covers 1 to 8 consecutive tiles and some document covers exactly 8.
All inputs are finite; a program needn't handle non-finite values.
Results may differ from a plain program's by a relative error of at most 0.014.
Values may be sent and summed in bfloat16 or wider, within the bound.
No kernel may reach another device: no remote copies, remote signals or barrier semaphores. Data moves between devices by JAX's collectives and lax.ppermute only.
A program may use at most 256 MiB of HBM per device.

v0:
```python
import functools

import jax
import jax.numpy as jnp
from jax import lax
from jax.experimental import pallas as pl
from jax.experimental.pallas import tpu as pltpu
from jax.sharding import PartitionSpec as P

LATENT = 512
NOPE = 128
ROPE = 64
VDIM = 128
HEADS = 32
TILE = 128
QDIM = NOPE + ROPE
KVDIM = NOPE + VDIM
WIDE = LATENT + ROPE
STEP_HEADS = 4
CHUNKS = ((0, 4), (4, 4))
BF16 = jnp.bfloat16
F32 = jnp.float32

ROWS_ROWS = (((1,), (1,)), ((), ()))
COLS_COLS = (((0,), (0,)), ((), ()))


def dot(a, b):
    return jnp.dot(a, b, preferred_element_type=F32)


def dot_general(a, b, dims):
    return lax.dot_general(a, b, dims, preferred_element_type=F32)


def attend_kernel(core_ref, keys_ref, bias_ref, q_ref, g_ref, w_ref, *rest, scale, is_first, is_last):
    att_ref, gq_ref, keep_ref, send_ref, dkeys_ref = rest[-6:-1]
    acc_ref = rest[-1]
    tok = q_ref.shape[0]
    keys = keys_ref[...]
    latent = keys_ref[:, :LATENT]
    q_nope, q_cat, g_heads, g_abs = [], [], [], []
    for h in range(STEP_HEADS):
        qn = q_ref[:, h * QDIM:h * QDIM + NOPE]
        qr = q_ref[:, h * QDIM + NOPE:(h + 1) * QDIM]
        g = g_ref[:, h * VDIM:(h + 1) * VDIM]
        wk = w_ref[:, h * KVDIM:h * KVDIM + NOPE]
        wv = w_ref[:, h * KVDIM + NOPE:(h + 1) * KVDIM]
        qa = (dot_general(qn, wk, ROWS_ROWS) * scale).astype(BF16)
        qr = (qr.astype(F32) * scale).astype(BF16)
        q_nope.append(qn)
        q_cat.append(jnp.concatenate([qa, qr], axis=1))
        g_heads.append(g)
        g_abs.append(dot_general(g, wv, ROWS_ROWS).astype(BF16))
    q_cat = jnp.concatenate(q_cat, axis=0)
    g_abs = jnp.concatenate(g_abs, axis=0)
    scores = dot_general(q_cat, keys, ROWS_ROWS)
    grad_probs = dot_general(g_abs, latent, ROWS_ROWS)
    bias = bias_ref[...]
    probs_half, grad_scores = [], []
    for h in range(STEP_HEADS):
        s = scores[h * tok:(h + 1) * tok] + bias
        s = jnp.exp(s - jnp.max(s, axis=1, keepdims=True))
        p = s * (1.0 / jnp.sum(s, axis=1, keepdims=True))
        gp = grad_probs[h * tok:(h + 1) * tok]
        row_dot = jnp.sum(p * gp, axis=1, keepdims=True)
        probs_half.append(p.astype(BF16))
        grad_scores.append((p * (gp - row_dot)).astype(BF16))
    probs_half = jnp.concatenate(probs_half, axis=0)
    grad_scores = jnp.concatenate(grad_scores, axis=0)

    @pl.when(pl.program_id(0) == 0)
    def _():
        acc_ref[...] = jnp.zeros_like(acc_ref) if is_first else rest[0][...]

    acc_ref[:LATENT] += dot_general(q_cat[:, :LATENT], grad_scores, COLS_COLS) + dot_general(
        g_abs, probs_half, COLS_COLS
    )
    acc_ref[LATENT:] += dot_general(q_cat[:, LATENT:], grad_scores, COLS_COLS)
    mixed = dot(probs_half, latent).astype(BF16)
    grad_mixed = dot(grad_scores, keys) * scale
    grad_mixed_lat = grad_mixed[:, :LATENT].astype(BF16)
    grad_rope = grad_mixed[:, LATENT:].astype(BF16)
    terms = []
    for h in range(STEP_HEADS):
        rows = slice(h * tok, (h + 1) * tok)
        wk = w_ref[:, h * KVDIM:h * KVDIM + NOPE]
        wv = w_ref[:, h * KVDIM + NOPE:(h + 1) * KVDIM]
        att_ref[:, h * VDIM:(h + 1) * VDIM] = dot(mixed[rows], wv).astype(BF16)
        gq_ref[:, h * QDIM:h * QDIM + NOPE] = dot(grad_mixed_lat[rows], wk).astype(BF16)
        gq_ref[:, h * QDIM + NOPE:(h + 1) * QDIM] = grad_rope[rows]
        key_term = dot_general(q_nope[h], grad_mixed_lat[rows], COLS_COLS).astype(BF16)
        value_term = dot_general(g_heads[h], mixed[rows], COLS_COLS).astype(BF16)
        terms.append((key_term, value_term))

    def put(ref, heads):
        for n, head in enumerate(heads):
            ref[n * KVDIM:n * KVDIM + NOPE] = terms[head][0]
            ref[n * KVDIM + NOPE:(n + 1) * KVDIM] = terms[head][1]

    @pl.when(core_ref[0] == 0)
    def _():
        put(keep_ref, (0, 1))
        put(send_ref, (2, 3))

    @pl.when(core_ref[0] != 0)
    def _():
        put(keep_ref, (2, 3))
        put(send_ref, (0, 1))

    @pl.when(pl.program_id(0) == pl.num_programs(0) - 1)
    def _():
        if is_last:
            dkeys_ref[...] = acc_ref[...].T.astype(BF16)
        else:
            dkeys_ref[...] = acc_ref[...]


def attend_chunk(core, keys, bias, queries, grad_out, kv_weight, held, first, count, scale):
    tok = queries.shape[0]
    n_keys = keys.shape[0]
    is_first, is_last = first == 0, (first + count) * STEP_HEADS == HEADS
    whole = lambda s, c: (0, 0)
    column = lambda s, c: (0, first + s)
    block = lambda s, c: (lax.rem(s + count - c[1], count), 0)
    heads = count * STEP_HEADS
    parts_shape = jax.ShapeDtypeStruct((count * 2 * KVDIM, LATENT), BF16)
    parts_spec = pl.BlockSpec((2 * KVDIM, LATENT), block)
    dkeys_shape = (n_keys, WIDE) if is_last else (WIDE, n_keys)
    held_specs = [
        pl.BlockSpec((WIDE, n_keys), whole),
        pl.BlockSpec(memory_space=pl.ANY),
        pl.BlockSpec(memory_space=pl.ANY),
    ]
    att, gq, keep, send, dkeys = pl.pallas_call(
        functools.partial(attend_kernel, scale=scale, is_first=is_first, is_last=is_last),
        grid_spec=pltpu.PrefetchScalarGridSpec(
            num_scalar_prefetch=1,
            grid=(count,),
            in_specs=[
                pl.BlockSpec((n_keys, WIDE), whole),
                pl.BlockSpec((tok, n_keys), whole),
                pl.BlockSpec((tok, STEP_HEADS * QDIM), column),
                pl.BlockSpec((tok, STEP_HEADS * VDIM), column),
                pl.BlockSpec((LATENT, STEP_HEADS * KVDIM), column),
            ] + held_specs[:len(held)],
            out_specs=[
                pl.BlockSpec((tok, STEP_HEADS * VDIM), column),
                pl.BlockSpec((tok, STEP_HEADS * QDIM), column),
                parts_spec,
                parts_spec,
                pl.BlockSpec(dkeys_shape, whole),
            ],
            scratch_shapes=[pltpu.VMEM((WIDE, n_keys), F32)],
        ),
        out_shape=[
            jax.ShapeDtypeStruct((tok, HEADS * VDIM), BF16),
            jax.ShapeDtypeStruct((tok, HEADS * QDIM), BF16),
            parts_shape,
            parts_shape,
            jax.ShapeDtypeStruct(dkeys_shape, BF16 if is_last else F32),
        ],
        input_output_aliases={7: 0, 8: 1} if held else {},
        compiler_params=pltpu.CompilerParams(vmem_limit_bytes=56 * 1024 * 1024),
        cost_estimate=pl.CostEstimate(
            flops=heads * 1_000_000_000, bytes_accessed=heads * 1_000_000, transcendentals=0
        ),
        name="attend",
    )(core, keys, bias, queries, grad_out, kv_weight, *held)
    return (dkeys, att, gq), keep, send


def table_lookup(lookup_table, positions):
    hits = positions[:, None] == jnp.arange(lookup_table.shape[0], dtype=jnp.int32)[None, :]
    return jnp.sum(jnp.where(hits, lookup_table[None, :], 0), axis=1)


def shifted(shard, axis, by):
    length = lax.axis_size(axis)
    pairs = [(i, i + by) for i in range(length) if 0 <= i + by < length]
    return lax.ppermute(shard, axis, pairs)


def body(queries, compressed, kv_weight, segments, grad_out):
    scale = QDIM ** (-0.5)
    tok = queries.shape[0]
    group = lax.axis_size("inner")
    n_outer = lax.axis_size("outer")
    inner = lax.axis_index("inner")
    outer = lax.axis_index("outer")
    own_block = outer * group + inner
    core = lax.rem(outer, 2)
    slots = jnp.arange(group, dtype=jnp.int32)
    earlier = shifted(compressed, "outer", 1)
    outgoing = jnp.where((slots >= inner)[:, None, None], compressed[None], earlier[None])
    gathered = lax.all_to_all(outgoing, "inner", split_axis=0, concat_axis=0, tiled=True)
    keys = gathered.reshape(group * tok, WIDE)
    key_block = jnp.where(slots <= inner, outer * group + slots, (outer - 1) * group + slots)
    seg_keys = table_lookup(segments, key_block)
    seg_query = table_lookup(segments, own_block[None])
    slot_ok = (seg_keys == seg_query) & (key_block >= 0)
    at = jnp.arange(tok, dtype=jnp.int32)
    allowed = slot_ok[None, :, None] & (
        (slots != inner)[None, :, None] | (at[None, None, :] <= at[:, None, None])
    )
    bias = jnp.where(allowed, 0.0, -1e30).astype(F32).reshape(tok, group * tok)

    swap = [(o, o ^ 1) for o in range(n_outer)]
    row_y = lax.rem(lax.div(outer, 2), 4)

    def along_y(shard, by):
        return lax.ppermute(
            shard, "outer", [(o, o // 8 * 8 + (o % 8 + 2 * by) % 8) for o in range(n_outer)]
        )

    def summed(keep, send):
        other = lax.ppermute(send, "outer", swap)
        return (keep.astype(F32) + other.astype(F32)).astype(BF16)

    which = jnp.stack([core, jnp.zeros_like(core)])
    held, keep, send = attend_chunk(
        which, keys, bias, queries, grad_out, kv_weight, (), 0, 4, scale
    )
    pair = summed(keep, send)
    which, pair = lax.optimization_barrier((jnp.stack([core, row_y]), pair))
    same_xc = [[x * 8 + y * 2 + c for y in range(4)] for x in range(2) for c in range(2)]
    first = lax.all_to_all(
        pair.reshape(4, 512, LATENT), "outer", split_axis=0, concat_axis=0,
        axis_index_groups=same_xc, tiled=True,
    )
    held, keep, send = attend_chunk(
        which, keys, bias, queries, grad_out, kv_weight, held, 4, 4, scale
    )
    held, keep, send, first = lax.optimization_barrier((held, keep, send, first))
    first = jnp.sum(first.astype(F32), axis=0).astype(BF16)
    dkeys, attended, grad_query = held
    pair = summed(keep, send).reshape(4, 512, LATENT)
    second = sum(along_y(pair[by], by).astype(F32) for by in range(1, 4))
    second = (second + pair[0].astype(F32)).astype(BF16)
    reduced = [first, second]
    dkeys = dkeys.reshape(group, tok, WIDE)
    arrived = lax.all_to_all(dkeys, "inner", split_axis=0, concat_axis=0, tiled=True).astype(F32)
    from_group = (slots >= inner)[:, None, None]
    own_term = jnp.sum(jnp.where(from_group, arrived, 0.0), axis=0)
    later_term = jnp.sum(jnp.where(from_group, 0.0, arrived), axis=0)
    next_term = shifted(later_term.astype(BF16), "outer", -1).astype(F32)
    grad_compressed = (own_term + next_term).astype(BF16)

    rest = [
        [(x * 8 + y * 2 + c) * group + i for x in range(2) for i in range(group)]
        for y in range(4) for c in range(2)
    ]
    reduced = jnp.concatenate(reduced, axis=0).reshape(16, 64, LATENT)
    last = lax.all_to_all(
        reduced, ("outer", "inner"), split_axis=0, concat_axis=0, axis_index_groups=rest, tiled=True
    )
    grad_weight_t = jnp.sum(last.astype(F32), axis=0)
    return attended, grad_query, grad_compressed, grad_weight_t


def solution(mesh):
    return jax.shard_map(
        body,
        mesh=mesh,
        in_specs=(
            P(("outer", "inner"), None),
            P(("outer", "inner"), None),
            P(),
            P(),
            P(("outer", "inner"), None),
        ),
        out_specs=(
            P(("outer", "inner"), None),
            P(("outer", "inner"), None),
            P(("outer", "inner"), None),
            P(("outer", "inner"), None),
        ),
        check_vma=False,
    )
```

profile of v0, /device:TPU:0, one launch (start us, length us, event | category | flops | bytes accessed | tf_op | source)
XLA Modules:
  0.0 169.7 jit_solution(8054455653807041028)
XLA Ops:
  0.6 1.3 collective-permute-start
  3.1 2.1 %broadcast_select_fusion = bf16[8,128,576]{1,2,0:T(8,128)(2,1)} fusion(pred[8]{0:T(512)(128)(4,1)S(1)} %iota_compare_fusion.3, bf16[128,576]{0,1:T(8,128)(2,1)S(1)} %collective-permute-done, bf16[128,576]{0,1:T(8,128)(2,1)} %param.6), kind=kLoop, calls=%fused_computation.7 | loop fusion | flops 589824 | bytes 1474568 | tf_op jit(solution)/shard_map/jit(_where)/select_n | solution.py:195
  5.2 8.3 %all-to-all-start = ((bf16[8,128,576]{1,2,0:T(8,128)(2,1)}), bf16[8,128,576]{1,2,0:T(8,128)(2,1)S(1)}, u32[]{:S(2)}, u32[]{:S(2)}) async-start(bf16[8,128,576]{1,2,0:T(8,128)(2,1)} %broadcast_select_fusion), calls=%async_computation | async-start | bytes 2359296 | tf_op jit(solution)/shard_map/all_to_all | solution.py:196
  16.1 13.5 %all-to-all-done = bf16[8,128,576]{1,2,0:T(8,128)(2,1)S(1)} async-done(((bf16[8,128,576]{1,2,0:T(8,128)(2,1)}), bf16[8,128,576]{1,2,0:T(8,128)(2,1)S(1)}, u32[]{:S(2)}, u32[]{:S(2)}) %all-to-all-start) | async-done | bytes 1179680 | tf_op jit(solution)/shard_map/all_to_all | solution.py:196
  29.6 1.5 copy.18
  31.0 28.3 %attend.2 = (bf16[128,4096]{1,0:T(8,128)(2,1)}, bf16[128,6144]{1,0:T(8,128)(2,1)}, bf16[2048,512]{1,0:T(8,128)(2,1)}, bf16[2048,512]{1,0:T(8,128)(2,1)}, f32[576,1024]{1,0:T(8,128)}) custom-call(s32[2]{0:T(128)} %pad_add_fusion.1.core_ref, bf16[1024,576]{1,0:T(8,128)(2,1)} %bitcast.17, f32[128,1024]{1,0:T(8,128)} %fusion.3.bias_ref, ...), custom_call_target="tpu_custom_call" | custom-call | flops 16000000000 | bytes 16000000 | tf_op jit(solution)/shard_map/attend/pallas_call | solution.py:135
  59.3 2.3 %collective-permute-start.1 = (bf16[2048,512]{1,0:T(8,128)(2,1)}, bf16[2048,512]{1,0:T(8,128)(2,1)S(1)}, u32[]{:S(2)}, u32[]{:S(2)}) collective-permute-start(bf16[2048,512]{1,0:T(8,128)(2,1)} %get-tuple-element.23), channel_id=1, source_target_pairs={{0,8},{8,0},{16,24},{24,16},{32,40},{40,32},{48,56},{56,48},{64,72... | collective-permute-start | bytes 6291464 | tf_op jit(solution)/shard_map/ppermute | solution.py:217
  62.2 3.4 %collective-permute-done.1 = bf16[2048,512]{1,0:T(8,128)(2,1)S(1)} collective-permute-done((bf16[2048,512]{1,0:T(8,128)(2,1)}, bf16[2048,512]{1,0:T(8,128)(2,1)S(1)}, u32[]{:S(2)}, u32[]{:S(2)}) %collective-permute-start.1) | collective-permute-done | bytes 2097184 | tf_op jit(solution)/shard_map/ppermute | solution.py:217
  65.6 3.5 %add_convert_fusion.1 = bf16[2048,512]{1,0:T(8,128)(2,1)} fusion(bf16[2048,512]{1,0:T(8,128)(2,1)S(1)} %collective-permute-done.1, bf16[2048,512]{1,0:T(8,128)(2,1)} %get-tuple-element.22), kind=kLoop, calls=%fused_computation.1 | loop fusion | flops 4194304 | bytes 6291456 | tf_op jit(solution)/shard_map/convert_element_type | solution.py:218
  69.1 6.5 %all-to-all-start.1 = ((bf16[4,512,512]{2,1,0:T(8,128)(2,1)}), bf16[4,512,512]{2,1,0:T(8,128)(2,1)S(1)}, u32[]{:S(2)}, u32[]{:S(2)}) async-start(bf16[4,512,512]{2,1,0:T(8,128)(2,1)} %bitcast.5), calls=%async_computation.1 | async-start | bytes 4194304 | tf_op jit(solution)/shard_map/all_to_all | solution.py:227
  75.7 28.9 %attend.3 = (bf16[128,4096]{1,0:T(8,128)(2,1)}, bf16[128,6144]{1,0:T(8,128)(2,1)}, bf16[2048,512]{1,0:T(8,128)(2,1)}, bf16[2048,512]{1,0:T(8,128)(2,1)}, bf16[1024,576]{1,0:T(8,128)(2,1)}) custom-call(s32[2]{0:T(128)} %pad_add_fusion.core_ref, bf16[1024,576]{1,0:T(8,128)(2,1)} %bitcast.18, ...), custom_call_target="tpu_custom_call", output_to_operand_aliasing={{0}: (7, {}), {1}: (8, {})} | custom-call | flops 16000000000 | bytes 16000000 | tf_op jit(solution)/shard_map/attend/pallas_call | solution.py:135
  104.7 3.0 %copy.19 = bf16[8,128,576]{1,2,0:T(8,128)(2,1)} copy(bf16[8,128,576]{2,1,0:T(8,128)(2,1)} %bitcast.19) | data formatting | bytes 2359296 | tf_op jit(solution)/shard_map/reshape | solution.py:241
  107.7 4.3 %all-to-all-start.2 = ((bf16[8,128,576]{1,2,0:T(8,128)(2,1)}), bf16[8,128,576]{1,2,0:T(8,128)(2,1)S(1)}, u32[]{:S(2)}, u32[]{:S(2)}) async-start(bf16[8,128,576]{1,2,0:T(8,128)(2,1)} %copy.19), calls=%async_computation.2 | async-start | bytes 2359296 | tf_op jit(solution)/shard_map/all_to_all | solution.py:242
  111.9 2.8 %add_convert_fusion = bf16[2048,512]{1,0:T(8,128)(2,1)S(1)} fusion(bf16[2048,512]{1,0:T(8,128)(2,1)} %collective-permute-done.3, bf16[2048,512]{1,0:T(8,128)(2,1)} %get-tuple-element.38), kind=kLoop, calls=%fused_computation | loop fusion | flops 4194304 | bytes 6291456 | tf_op jit(solution)/shard_map/convert_element_type | solution.py:218
  115.9 2.0 %collective-permute-start.4 = (bf16[512,512]{1,0:T(8,128)(2,1)}, bf16[512,512]{1,0:T(8,128)(2,1)}, u32[]{:S(2)}, u32[]{:S(2)}) collective-permute-start(bf16[512,512]{1,0:T(8,128)(2,1)} %get-tuple-element.50), channel_id=1, source_target_pairs={{0,16},{8,24},{16,32},{24,40},{32,48},{40,56},{48,0},{56,8},{64,80... | collective-permute-start | bytes 1572872 | tf_op jit(solution)/shard_map/ppermute | solution.py:212
  119.2 2.3 %collective-permute-start.5 = (bf16[512,512]{1,0:T(8,128)(2,1)}, bf16[512,512]{1,0:T(8,128)(2,1)}, u32[]{:S(2)}, u32[]{:S(2)}) collective-permute-start(bf16[512,512]{1,0:T(8,128)(2,1)} %get-tuple-element.52), channel_id=1, source_target_pairs={{0,32},{8,40},{16,48},{24,56},{32,0},{40,8},{48,16},{56,24},{64,96... | collective-permute-start | bytes 1572872 | tf_op jit(solution)/shard_map/ppermute | solution.py:212
  121.5 2.9 %reduce_sum.61 = bf16[512,512]{1,0:T(8,128)(2,1)} reduce(bf16[4,512,512]{2,1,0:T(8,128)(2,1)} %copy-done, bf16[]{:T(256)} %constant.34.clone.1), dimensions={0}, to_apply=%region_4.5 | reduce | flops 786432 | bytes 2621442 | tf_op jit(solution)/shard_map/reduce_sum | solution.py:235
  124.3 7.0 %collective-permute-done.4 = bf16[512,512]{1,0:T(8,128)(2,1)} collective-permute-done((bf16[512,512]{1,0:T(8,128)(2,1)}, bf16[512,512]{1,0:T(8,128)(2,1)}, u32[]{:S(2)}, u32[]{:S(2)}) %collective-permute-start.4) | collective-permute-done | bytes 524320 | tf_op jit(solution)/shard_map/ppermute | solution.py:212
  131.4 1.8 %collective-permute-done.6 = bf16[512,512]{1,0:T(8,128)(2,1)} collective-permute-done((bf16[512,512]{1,0:T(8,128)(2,1)}, bf16[512,512]{1,0:T(8,128)(2,1)}, u32[]{:S(2)}, u32[]{:S(2)}) %collective-permute-start.6) | collective-permute-done | bytes 524320 | tf_op jit(solution)/shard_map/ppermute | solution.py:212
  133.1 10.5 %collective-permute-done.5 = bf16[512,512]{1,0:T(8,128)(2,1)} collective-permute-done((bf16[512,512]{1,0:T(8,128)(2,1)}, bf16[512,512]{1,0:T(8,128)(2,1)}, u32[]{:S(2)}, u32[]{:S(2)}) %collective-permute-start.5) | collective-permute-done | bytes 524320 | tf_op jit(solution)/shard_map/ppermute | solution.py:212
  143.6 1.6 add_convert_fusion.2
  146.3 7.0 %all-to-all-start.3 = ((bf16[16,64,512]{2,1,0:T(8,128)(2,1)}), bf16[16,64,512]{2,1,0:T(8,128)(2,1)S(1)}, u32[]{:S(2)}, u32[]{:S(2)}) async-start(bf16[16,64,512]{2,1,0:T(8,128)(2,1)} %bitcast.7), calls=%async_computation.3 | async-start | bytes 2097152 | tf_op jit(solution)/shard_map/all_to_all | solution.py:254
  155.5 1.8 %collective-permute-done.2 = bf16[128,576]{1,0:T(8,128)(2,1)S(1)} collective-permute-done((bf16[128,576]{1,0:T(8,128)(2,1)S(1)}, bf16[128,576]{1,0:T(8,128)(2,1)S(1)}, u32[]{:S(2)}, u32[]{:S(2)}) %collective-permute-start.2) | collective-permute-done | bytes 147488 | tf_op jit(solution)/shard_map/ppermute | solution.py:181
  158.1 10.8 %all-to-all-done.3 = bf16[16,64,512]{2,1,0:T(8,128)(2,1)S(1)} async-done(((bf16[16,64,512]{2,1,0:T(8,128)(2,1)}), bf16[16,64,512]{2,1,0:T(8,128)(2,1)S(1)}, u32[]{:S(2)}, u32[]{:S(2)}) %all-to-all-start.3) | async-done | bytes 1048608 | tf_op jit(solution)/shard_map/all_to_all | solution.py:254
  (33 shorter events, 11.6 us)
Async XLA Ops:
  0.6 12.9 %copy-start.2 = (s32[128]{0:T(128)S(1)}, s32[128]{0:T(128)}, u32[]{:S(2)}) copy-start(s32[128]{0:T(128)} %param.8) | copy-start | bytes 1540
  0.6 2.5 %collective-permute-start = (bf16[128,576]{0,1:T(8,128)(2,1)}, bf16[128,576]{0,1:T(8,128)(2,1)S(1)}, u32[]{:S(2)}, u32[]{:S(2)}) collective-permute-start(bf16[128,576]{0,1:T(8,128)(2,1)} %param.6), channel_id=1, source_target_pairs={{0,8},{8,16},{16,24},{24,32},{32,40},{40,48},{48,56},{56,64},{64,7... | collective-permute-start | bytes 442376 | tf_op jit(solution)/shard_map/ppermute | solution.py:181
  5.2 24.3 %all-to-all-start = ((bf16[8,128,576]{1,2,0:T(8,128)(2,1)}), bf16[8,128,576]{1,2,0:T(8,128)(2,1)S(1)}, u32[]{:S(2)}, u32[]{:S(2)}) async-start(bf16[8,128,576]{1,2,0:T(8,128)(2,1)} %broadcast_select_fusion), calls=%async_computation | async-start | bytes 2359296 | tf_op jit(solution)/shard_map/all_to_all | solution.py:196
  59.3 6.3 %collective-permute-start.1 = (bf16[2048,512]{1,0:T(8,128)(2,1)}, bf16[2048,512]{1,0:T(8,128)(2,1)S(1)}, u32[]{:S(2)}, u32[]{:S(2)}) collective-permute-start(bf16[2048,512]{1,0:T(8,128)(2,1)} %get-tuple-element.23), channel_id=1, source_target_pairs={{0,8},{8,0},{16,24},{24,16},{32,40},{40,32},{48,56},{56,48},{64,72... | collective-permute-start | bytes 6291464 | tf_op jit(solution)/shard_map/ppermute | solution.py:217
  69.1 35.4 %all-to-all-start.1 = ((bf16[4,512,512]{2,1,0:T(8,128)(2,1)}), bf16[4,512,512]{2,1,0:T(8,128)(2,1)S(1)}, u32[]{:S(2)}, u32[]{:S(2)}) async-start(bf16[4,512,512]{2,1,0:T(8,128)(2,1)} %bitcast.5), calls=%async_computation.1 | async-start | bytes 4194304 | tf_op jit(solution)/shard_map/all_to_all | solution.py:227
  104.6 3.1 %copy-start = (bf16[4,512,512]{2,1,0:T(8,128)(2,1)}, bf16[4,512,512]{2,1,0:T(8,128)(2,1)S(1)}, u32[]{:S(2)}) copy-start(bf16[4,512,512]{2,1,0:T(8,128)(2,1)S(1)} %all-to-all-done.1) | copy-start | bytes 6291460
  104.6 7.4 %collective-permute-start.3 = (bf16[2048,512]{1,0:T(8,128)(2,1)}, bf16[2048,512]{1,0:T(8,128)(2,1)}, u32[]{:S(2)}, u32[]{:S(2)}) collective-permute-start(bf16[2048,512]{1,0:T(8,128)(2,1)} %get-tuple-element.39), channel_id=1, source_target_pairs={{0,8},{8,0},{16,24},{24,16},{32,40},{40,32},{48,56},{56,48},{64,72... | collective-permute-start | bytes 6291464 | tf_op jit(solution)/shard_map/ppermute | solution.py:217
  107.7 38.6 %all-to-all-start.2 = ((bf16[8,128,576]{1,2,0:T(8,128)(2,1)}), bf16[8,128,576]{1,2,0:T(8,128)(2,1)S(1)}, u32[]{:S(2)}, u32[]{:S(2)}) async-start(bf16[8,128,576]{1,2,0:T(8,128)(2,1)} %copy.19), calls=%async_computation.2 | async-start | bytes 2359296 | tf_op jit(solution)/shard_map/all_to_all | solution.py:242
  115.9 15.5 %collective-permute-start.4 = (bf16[512,512]{1,0:T(8,128)(2,1)}, bf16[512,512]{1,0:T(8,128)(2,1)}, u32[]{:S(2)}, u32[]{:S(2)}) collective-permute-start(bf16[512,512]{1,0:T(8,128)(2,1)} %get-tuple-element.50), channel_id=1, source_target_pairs={{0,16},{8,24},{16,32},{24,40},{32,48},{40,56},{48,0},{56,8},{64,80... | collective-permute-start | bytes 1572872 | tf_op jit(solution)/shard_map/ppermute | solution.py:212
  118.0 15.2 %collective-permute-start.6 = (bf16[512,512]{1,0:T(8,128)(2,1)}, bf16[512,512]{1,0:T(8,128)(2,1)}, u32[]{:S(2)}, u32[]{:S(2)}) collective-permute-start(bf16[512,512]{1,0:T(8,128)(2,1)} %get-tuple-element.51), channel_id=1, source_target_pairs={{0,48},{8,56},{16,0},{24,8},{32,16},{40,24},{48,32},{56,40},{64,11... | collective-permute-start | bytes 1572872 | tf_op jit(solution)/shard_map/ppermute | solution.py:212
  119.2 24.5 %collective-permute-start.5 = (bf16[512,512]{1,0:T(8,128)(2,1)}, bf16[512,512]{1,0:T(8,128)(2,1)}, u32[]{:S(2)}, u32[]{:S(2)}) collective-permute-start(bf16[512,512]{1,0:T(8,128)(2,1)} %get-tuple-element.52), channel_id=1, source_target_pairs={{0,32},{8,40},{16,48},{24,56},{32,0},{40,8},{48,16},{56,24},{64,96... | collective-permute-start | bytes 1572872 | tf_op jit(solution)/shard_map/ppermute | solution.py:212
  124.3 20.9 %copy-start.1 = (bf16[512,512]{1,0:T(8,128)(2,1)S(1)}, bf16[512,512]{1,0:T(8,128)(2,1)}, u32[]{:S(2)}) copy-start(bf16[512,512]{1,0:T(8,128)(2,1)} %reduce_sum.61) | copy-start | bytes 1572868
  146.3 22.6 %all-to-all-start.3 = ((bf16[16,64,512]{2,1,0:T(8,128)(2,1)}), bf16[16,64,512]{2,1,0:T(8,128)(2,1)S(1)}, u32[]{:S(2)}, u32[]{:S(2)}) async-start(bf16[16,64,512]{2,1,0:T(8,128)(2,1)} %bitcast.7), calls=%async_computation.3 | async-start | bytes 2097152 | tf_op jit(solution)/shard_map/all_to_all | solution.py:254
  154.0 3.3 %collective-permute-start.2 = (bf16[128,576]{1,0:T(8,128)(2,1)S(1)}, bf16[128,576]{1,0:T(8,128)(2,1)S(1)}, u32[]{:S(2)}, u32[]{:S(2)}) collective-permute-start(bf16[128,576]{1,0:T(8,128)(2,1)S(1)} %copy.24), channel_id=1, source_target_pairs={{8,0},{16,8},{24,16},{32,24},{40,32},{48,40},{56,48},{64,56},{72,6... | collective-permute-start | bytes 442376 | tf_op jit(solution)/shard_map/ppermute | solution.py:181
where the time goes:
time: 170 us
  Pallas kernels  57.2 us (34%)
  waiting for transfers between devices  49.4 us (29%)
  starting transfers between devices  36.6 us (22%)
  other arithmetic  18.9 us (11%)
  local copies, waits for them, and re-layouts  6.92 us (4%)
    pallas_call x2, Pallas kernels, attend_chunk(): pl.pallas_call(functools.partial(attend_kernel, scale=scale, is_first=is_...  57.2 us
    ppermute x3, waiting for transfers between devices, along_y(): lax.ppermute(shard, 'outer', [(o, o // 8 * 8 + (o % 8 + 2 * by) % 8) for...  19.3 us
    all_to_all x1, waiting for transfers between devices, body(): lax.all_to_all(outgoing, 'inner', split_axis=0, concat_axis=0, tiled=True)  13.5 us
    all_to_all x1, waiting for transfers between devices, body(): lax.all_to_all(reduced, ('outer', 'inner'), split_axis=0, concat_axis=0,...  10.8 us
    all_to_all x1, starting transfers between devices, body(): lax.all_to_all(outgoing, 'inner', split_axis=0, concat_axis=0, tiled=True)  8.31 us
    all_to_all x1, starting transfers between devices, body(): lax.all_to_all(reduced, ('outer', 'inner'), split_axis=0, concat_axis=0,...  7.03 us
    all_to_all x1, starting transfers between devices, body(): lax.all_to_all(pair.reshape(4, 512, LATENT), 'outer', split_axis=0, conca...  6.54 us
    convert_element_type x2, other arithmetic, summed(): return (keep.astype(F32) + other.astype(F32)).astype(BF16)  6.36 us
  transfers between devices with their start and end apart: 11, of which 8 were waited for; matrix products, arithmetic and copies ran while one was open for 11% of the time, Pallas kernels for 17%

commit v1 on v0

--- a/solution.py
+++ b/solution.py
@@ -34,28 +34,41 @@
 
 
 def attend_kernel(core_ref, keys_ref, bias_ref, q_ref, g_ref, w_ref, *rest, scale, is_first, is_last):
-    att_ref, gq_ref, keep_ref, send_ref, dkeys_ref = rest[-6:-1]
-    acc_ref = rest[-1]
+    att_ref, gq_ref, keep_ref, send_ref, dkeys_ref, keys_t_ref, *acc = rest if is_first else rest[3:]
+    acc_ref = acc[0] if is_last else dkeys_ref
     tok = q_ref.shape[0]
-    keys = keys_ref[...]
-    latent = keys_ref[:, :LATENT]
-    q_nope, q_cat, g_heads, g_abs = [], [], [], []
+    slots = keys_ref.shape[0]
+
+    @pl.when(pl.program_id(0) == 0)
+    def _():
+        acc_ref[...] = jnp.zeros_like(acc_ref) if is_first else rest[0][...]
+        for s in range(slots):
+            keys_t_ref[:, s * tok:(s + 1) * tok] = keys_ref[s]
+
+    def q_nope(h):
+        return q_ref[:, h * QDIM:h * QDIM + NOPE]
+
+    def grad_head(h):
+        return g_ref[:, h * VDIM:(h + 1) * VDIM]
+
+    def key_weight(h):
+        return w_ref[:, h * KVDIM:h * KVDIM + NOPE]
+
+    def value_weight(h):
+        return w_ref[:, h * KVDIM + NOPE:(h + 1) * KVDIM]
+
+    keys_t = keys_t_ref[...]
+    latent_t = keys_t_ref[:LATENT]
+    q_cat, g_abs = [], []
     for h in range(STEP_HEADS):
-        qn = q_ref[:, h * QDIM:h * QDIM + NOPE]
-        qr = q_ref[:, h * QDIM + NOPE:(h + 1) * QDIM]
-        g = g_ref[:, h * VDIM:(h + 1) * VDIM]
-        wk = w_ref[:, h * KVDIM:h * KVDIM + NOPE]
-        wv = w_ref[:, h * KVDIM + NOPE:(h + 1) * KVDIM]
-        qa = (dot_general(qn, wk, ROWS_ROWS) * scale).astype(BF16)
-        qr = (qr.astype(F32) * scale).astype(BF16)
-        q_nope.append(qn)
+        qa = (dot_general(q_nope(h), key_weight(h), ROWS_ROWS) * scale).astype(BF16)
+        qr = (q_ref[:, h * QDIM + NOPE:(h + 1) * QDIM].astype(F32) * scale).astype(BF16)
         q_cat.append(jnp.concatenate([qa, qr], axis=1))
-        g_heads.append(g)
-        g_abs.append(dot_general(g, wv, ROWS_ROWS).astype(BF16))
+        g_abs.append(dot_general(grad_head(h), value_weight(h), ROWS_ROWS).astype(BF16))
     q_cat = jnp.concatenate(q_cat, axis=0)
     g_abs = jnp.concatenate(g_abs, axis=0)
-    scores = dot_general(q_cat, keys, ROWS_ROWS)
-    grad_probs = dot_general(g_abs, latent, ROWS_ROWS)
+    scores = dot(q_cat, keys_t)
+    grad_probs = dot(g_abs, latent_t)
     bias = bias_ref[...]
     probs_half, grad_scores = [], []
     for h in range(STEP_HEADS):
@@ -68,29 +81,22 @@
         grad_scores.append((p * (gp - row_dot)).astype(BF16))
     probs_half = jnp.concatenate(probs_half, axis=0)
     grad_scores = jnp.concatenate(grad_scores, axis=0)
-
-    @pl.when(pl.program_id(0) == 0)
-    def _():
-        acc_ref[...] = jnp.zeros_like(acc_ref) if is_first else rest[0][...]
-
     acc_ref[:LATENT] += dot_general(q_cat[:, :LATENT], grad_scores, COLS_COLS) + dot_general(
         g_abs, probs_half, COLS_COLS
     )
     acc_ref[LATENT:] += dot_general(q_cat[:, LATENT:], grad_scores, COLS_COLS)
-    mixed = dot(probs_half, latent).astype(BF16)
-    grad_mixed = dot(grad_scores, keys) * scale
+    mixed = dot_general(probs_half, latent_t, ROWS_ROWS).astype(BF16)
+    grad_mixed = dot_general(grad_scores, keys_t, ROWS_ROWS) * scale
     grad_mixed_lat = grad_mixed[:, :LATENT].astype(BF16)
     grad_rope = grad_mixed[:, LATENT:].astype(BF16)
     terms = []
     for h in range(STEP_HEADS):
         rows = slice(h * tok, (h + 1) * tok)
-        wk = w_ref[:, h * KVDIM:h * KVDIM + NOPE]
-        wv = w_ref[:, h * KVDIM + NOPE:(h + 1) * KVDIM]
-        att_ref[:, h * VDIM:(h + 1) * VDIM] = dot(mixed[rows], wv).astype(BF16)
-        gq_ref[:, h * QDIM:h * QDIM + NOPE] = dot(grad_mixed_lat[rows], wk).astype(BF16)
+        att_ref[:, h * VDIM:(h + 1) * VDIM] = dot(mixed[rows], value_weight(h)).astype(BF16)
+        gq_ref[:, h * QDIM:h * QDIM + NOPE] = dot(grad_mixed_lat[rows], key_weight(h)).astype(BF16)
         gq_ref[:, h * QDIM + NOPE:(h + 1) * QDIM] = grad_rope[rows]
-        key_term = dot_general(q_nope[h], grad_mixed_lat[rows], COLS_COLS).astype(BF16)
-        value_term = dot_general(g_heads[h], mixed[rows], COLS_COLS).astype(BF16)
+        key_term = dot_general(q_nope(h), grad_mixed_lat[rows], COLS_COLS).astype(BF16)
+        value_term = dot_general(grad_head(h), mixed[rows], COLS_COLS).astype(BF16)
         terms.append((key_term, value_term))
 
     def put(ref, heads):
@@ -108,17 +114,17 @@
         put(keep_ref, (2, 3))
         put(send_ref, (0, 1))
 
-    @pl.when(pl.program_id(0) == pl.num_programs(0) - 1)
-    def _():
-        if is_last:
-            dkeys_ref[...] = acc_ref[...].T.astype(BF16)
-        else:
-            dkeys_ref[...] = acc_ref[...]
+    if is_last:
+        @pl.when(pl.program_id(0) == pl.num_programs(0) - 1)
+        def _():
+            for s in range(slots):
+                dkeys_ref[s] = acc_ref[:, s * tok:(s + 1) * tok].astype(BF16)
 
 
 def attend_chunk(core, keys, bias, queries, grad_out, kv_weight, held, first, count, scale):
     tok = queries.shape[0]
-    n_keys = keys.shape[0]
+    slots = keys.shape[0]
+    n_keys = slots * tok
     is_first, is_last = first == 0, (first + count) * STEP_HEADS == HEADS
     whole = lambda s, c: (0, 0)
     column = lambda s, c: (0, first + s)
@@ -126,7 +132,8 @@
     heads = count * STEP_HEADS
     parts_shape = jax.ShapeDtypeStruct((count * 2 * KVDIM, LATENT), BF16)
     parts_spec = pl.BlockSpec((2 * KVDIM, LATENT), block)
-    dkeys_shape = (n_keys, WIDE) if is_last else (WIDE, n_keys)
+    dkeys_shape = keys.shape if is_last else (WIDE, n_keys)
+    whole3 = lambda s, c: (0, 0, 0)
     held_specs = [
         pl.BlockSpec((WIDE, n_keys), whole),
         pl.BlockSpec(memory_space=pl.ANY),
@@ -138,7 +145,7 @@
             num_scalar_prefetch=1,
             grid=(count,),
             in_specs=[
-                pl.BlockSpec((n_keys, WIDE), whole),
+                pl.BlockSpec(keys.shape, whole3),
                 pl.BlockSpec((tok, n_keys), whole),
                 pl.BlockSpec((tok, STEP_HEADS * QDIM), column),
                 pl.BlockSpec((tok, STEP_HEADS * VDIM), column),
@@ -149,9 +156,10 @@
                 pl.BlockSpec((tok, STEP_HEADS * QDIM), column),
                 parts_spec,
                 parts_spec,
-                pl.BlockSpec(dkeys_shape, whole),
+                pl.BlockSpec(dkeys_shape, whole3 if is_last else whole),
             ],
-            scratch_shapes=[pltpu.VMEM((WIDE, n_keys), F32)],
+            scratch_shapes=[pltpu.VMEM((WIDE, n_keys), BF16)]
+            + [pltpu.VMEM((WIDE, n_keys), F32)] * is_last,
         ),
         out_shape=[
             jax.ShapeDtypeStruct((tok, HEADS * VDIM), BF16),
@@ -191,10 +199,10 @@
     own_block = outer * group + inner
     core = lax.rem(outer, 2)
     slots = jnp.arange(group, dtype=jnp.int32)
-    earlier = shifted(compressed, "outer", 1)
-    outgoing = jnp.where((slots >= inner)[:, None, None], compressed[None], earlier[None])
-    gathered = lax.all_to_all(outgoing, "inner", split_axis=0, concat_axis=0, tiled=True)
-    keys = gathered.reshape(group * tok, WIDE)
+    own = compressed.T
+    earlier = shifted(own, "outer", 1)
+    outgoing = jnp.where((slots >= inner)[:, None, None], own[None], earlier[None])
+    keys = lax.all_to_all(outgoing, "inner", split_axis=0, concat_axis=0, tiled=True)
     key_block = jnp.where(slots <= inner, outer * group + slots, (outer - 1) * group + slots)
     seg_keys = table_lookup(segments, key_block)
     seg_query = table_lookup(segments, own_block[None])
@@ -238,13 +246,12 @@
     second = sum(along_y(pair[by], by).astype(F32) for by in range(1, 4))
     second = (second + pair[0].astype(F32)).astype(BF16)
     reduced = [first, second]
-    dkeys = dkeys.reshape(group, tok, WIDE)
     arrived = lax.all_to_all(dkeys, "inner", split_axis=0, concat_axis=0, tiled=True).astype(F32)
     from_group = (slots >= inner)[:, None, None]
     own_term = jnp.sum(jnp.where(from_group, arrived, 0.0), axis=0)
     later_term = jnp.sum(jnp.where(from_group, 0.0, arrived), axis=0)
     next_term = shifted(later_term.astype(BF16), "outer", -1).astype(F32)
-    grad_compressed = (own_term + next_term).astype(BF16)
+    grad_compressed = (own_term + next_term).astype(BF16).T
 
     rest = [
         [(x * 8 + y * 2 + c) * group + i for x in range(2) for i in range(group)]

time: 170 us -> 166 us (0.976)
  local copies, waits for them, and re-layouts: 6.92 us -> 2.37 us
  Pallas kernels: 57.2 us -> 55.2 us
  waiting for transfers between devices: 49.4 us -> 51.1 us
    reshape x1 -> x0, local copies, waits for them, and re-layouts: 3 us -> none  [body(): dkeys = dkeys.reshape(group, tok, WIDE)]
    pallas_call x2, Pallas kernels: 57.2 us -> 55.2 us  [attend_chunk(): pl.pallas_call(functools.partial(attend_kernel, scale=scale, is_first=is_...]
  transfers between devices with their start and end apart: 11 -> 11, of which waited for: 8 -> 9; matrix products, arithmetic and copies ran while one was open for 11% -> 9% of each run, Pallas kernels for 17% -> 17%
where the time goes in v1:
time: 166 us
  Pallas kernels  55.2 us (33%)
  waiting for transfers between devices  51.1 us (31%)
  starting transfers between devices  36.5 us (22%)
  other arithmetic  19.8 us (12%)
  local copies, waits for them, and re-layouts  2.37 us (1%)
    pallas_call x2, Pallas kernels, attend_chunk(): pl.pallas_call(functools.partial(attend_kernel, scale=scale, is_first=is_...  55.2 us
    ppermute x3, waiting for transfers between devices, along_y(): lax.ppermute(shard, 'outer', [(o, o // 8 * 8 + (o % 8 + 2 * by) % 8) for...  19.8 us
    all_to_all x1, waiting for transfers between devices, body(): lax.all_to_all(outgoing, 'inner', split_axis=0, concat_axis=0, tiled=True)  13.5 us
    all_to_all x1, waiting for transfers between devices, body(): lax.all_to_all(reduced, ('outer', 'inner'), split_axis=0, concat_axis=0,...  11.7 us
    all_to_all x1, starting transfers between devices, body(): lax.all_to_all(outgoing, 'inner', split_axis=0, concat_axis=0, tiled=True)  8.31 us
    all_to_all x1, starting transfers between devices, body(): lax.all_to_all(reduced, ('outer', 'inner'), split_axis=0, concat_axis=0,...  6.9 us
    all_to_all x1, starting transfers between devices, body(): lax.all_to_all(pair.reshape(4, 512, LATENT), 'outer', split_axis=0, conca...  6.55 us
    convert_element_type x2, other arithmetic, summed(): return (keep.astype(F32) + other.astype(F32)).astype(BF16)  6.48 us
  transfers between devices with their start and end apart: 11, of which 9 were waited for; matrix products, arithmetic and copies ran while one was open for 9% of the time, Pallas kernels for 17%

profile of v1, /device:TPU:0, one launch (start us, length us, event | category | flops | bytes accessed | tf_op | source)
XLA Modules:
  0.0 165.7 jit_solution(10011788609518640996)
XLA Ops:
  0.6 1.3 collective-permute-start
  3.1 2.1 %broadcast_select_fusion = bf16[8,576,128]{2,1,0:T(8,128)(2,1)} fusion(pred[8]{0:T(512)(128)(4,1)S(1)} %iota_compare_fusion.3, bf16[576,128]{1,0:T(8,128)(2,1)S(1)} %collective-permute-done, bf16[576,128]{1,0:T(8,128)(2,1)} %bitcast.20), kind=kLoop, calls=%fused_computation.7 | loop fusion | flops 589824 | bytes 1474568 | tf_op jit(solution)/shard_map/jit(_where)/select_n | solution.py:204
  5.2 8.3 %all-to-all-start = ((bf16[8,576,128]{2,1,0:T(8,128)(2,1)}), bf16[8,576,128]{2,1,0:T(8,128)(2,1)S(1)}, u32[]{:S(2)}, u32[]{:S(2)}) async-start(bf16[8,576,128]{2,1,0:T(8,128)(2,1)} %broadcast_select_fusion), calls=%async_computation | async-start | bytes 2359296 | tf_op jit(solution)/shard_map/all_to_all | solution.py:205
  16.1 13.5 %all-to-all-done.keys_ref = bf16[8,576,128]{2,1,0:T(8,128)(2,1)S(1)} async-done(((bf16[8,576,128]{2,1,0:T(8,128)(2,1)}), bf16[8,576,128]{2,1,0:T(8,128)(2,1)S(1)}, u32[]{:S(2)}, u32[]{:S(2)}) %all-to-all-start) | async-done | bytes 1179680 | tf_op jit(solution)/shard_map/all_to_all | solution.py:205
  30.6 27.3 %attend.2 = (bf16[128,4096]{1,0:T(8,128)(2,1)}, bf16[128,6144]{1,0:T(8,128)(2,1)}, bf16[2048,512]{1,0:T(8,128)(2,1)}, bf16[2048,512]{1,0:T(8,128)(2,1)}, f32[576,1024]{1,0:T(8,128)}) custom-call(s32[2]{0:T(128)} %pad_add_fusion.1.core_ref, bf16[8,576,128]{2,1,0:T(8,128)(2,1)} %copy-done.2, f32[128,1024]{1,0:T(8,128)} %fusion.3.bias_ref, ...), custom_call_target="tpu_custom_call" | custom-call | flops 16000000000 | bytes 16000000 | tf_op jit(solution)/shard_map/attend/pallas_call | solution.py:142
  57.9 2.3 %collective-permute-start.1 = (bf16[2048,512]{1,0:T(8,128)(2,1)}, bf16[2048,512]{1,0:T(8,128)(2,1)S(1)}, u32[]{:S(2)}, u32[]{:S(2)}) collective-permute-start(bf16[2048,512]{1,0:T(8,128)(2,1)} %get-tuple-element.23), channel_id=1, source_target_pairs={{0,8},{8,0},{16,24},{24,16},{32,40},{40,32},{48,56},{56,48},{64,72... | collective-permute-start | bytes 6291464 | tf_op jit(solution)/shard_map/ppermute | solution.py:225
  60.8 3.4 %collective-permute-done.1 = bf16[2048,512]{1,0:T(8,128)(2,1)S(1)} collective-permute-done((bf16[2048,512]{1,0:T(8,128)(2,1)}, bf16[2048,512]{1,0:T(8,128)(2,1)S(1)}, u32[]{:S(2)}, u32[]{:S(2)}) %collective-permute-start.1) | collective-permute-done | bytes 2097184 | tf_op jit(solution)/shard_map/ppermute | solution.py:225
  64.2 3.7 %add_convert_fusion.1 = bf16[2048,512]{1,0:T(8,128)(2,1)} fusion(bf16[2048,512]{1,0:T(8,128)(2,1)S(1)} %collective-permute-done.1, bf16[2048,512]{1,0:T(8,128)(2,1)} %get-tuple-element.22), kind=kLoop, calls=%fused_computation.1 | loop fusion | flops 4194304 | bytes 6291456 | tf_op jit(solution)/shard_map/convert_element_type | solution.py:226
  67.9 6.5 %all-to-all-start.1 = ((bf16[4,512,512]{2,1,0:T(8,128)(2,1)}), bf16[4,512,512]{2,1,0:T(8,128)(2,1)S(1)}, u32[]{:S(2)}, u32[]{:S(2)}) async-start(bf16[4,512,512]{2,1,0:T(8,128)(2,1)} %bitcast.5), calls=%async_computation.1 | async-start | bytes 4194304 | tf_op jit(solution)/shard_map/all_to_all | solution.py:235
  74.4 27.9 %attend.3 = (bf16[128,4096]{1,0:T(8,128)(2,1)}, bf16[128,6144]{1,0:T(8,128)(2,1)}, bf16[2048,512]{1,0:T(8,128)(2,1)}, bf16[2048,512]{1,0:T(8,128)(2,1)}, bf16[8,576,128]{2,1,0:T(8,128)(2,1)}) custom-call(s32[2]{0:T(128)} %pad_add_fusion.core_ref, bf16[8,576,128]{2,1,0:T(8,128)(2,1)} %copy-done.2, ...), custom_call_target="tpu_custom_call", output_to_operand_aliasing={{0}: (7, {}), {1}: (8, {})} | custom-call | flops 16000000000 | bytes 16000000 | tf_op jit(solution)/shard_map/attend/pallas_call | solution.py:142
  102.4 4.3 %all-to-all-start.2 = ((bf16[8,576,128]{2,1,0:T(8,128)(2,1)}), bf16[8,576,128]{2,1,0:T(8,128)(2,1)S(1)}, u32[]{:S(2)}, u32[]{:S(2)}) async-start(bf16[8,576,128]{2,1,0:T(8,128)(2,1)} %get-tuple-element.36), calls=%async_computation.2 | async-start | bytes 2359296 | tf_op jit(solution)/shard_map/all_to_all | solution.py:249
  106.9 2.8 %add_convert_fusion = bf16[2048,512]{1,0:T(8,128)(2,1)S(1)} fusion(bf16[2048,512]{1,0:T(8,128)(2,1)} %collective-permute-done.3, bf16[2048,512]{1,0:T(8,128)(2,1)} %get-tuple-element.38), kind=kLoop, calls=%fused_computation | loop fusion | flops 4194304 | bytes 6291456 | tf_op jit(solution)/shard_map/convert_element_type | solution.py:226
  110.9 2.0 %collective-permute-start.4 = (bf16[512,512]{1,0:T(8,128)(2,1)}, bf16[512,512]{1,0:T(8,128)(2,1)}, u32[]{:S(2)}, u32[]{:S(2)}) collective-permute-start(bf16[512,512]{1,0:T(8,128)(2,1)} %get-tuple-element.42), channel_id=1, source_target_pairs={{0,16},{8,24},{16,32},{24,40},{32,48},{40,56},{48,0},{56,8},{64,80... | collective-permute-start | bytes 1572872 | tf_op jit(solution)/shard_map/ppermute | solution.py:220
  112.9 1.2 collective-permute-start.6
  114.1 2.3 %collective-permute-start.5 = (bf16[512,512]{1,0:T(8,128)(2,1)}, bf16[512,512]{1,0:T(8,128)(2,1)}, u32[]{:S(2)}, u32[]{:S(2)}) collective-permute-start(bf16[512,512]{1,0:T(8,128)(2,1)} %get-tuple-element.44), channel_id=1, source_target_pairs={{0,32},{8,40},{16,48},{24,56},{32,0},{40,8},{48,16},{56,24},{64,96... | collective-permute-start | bytes 1572872 | tf_op jit(solution)/shard_map/ppermute | solution.py:220
  116.4 2.9 %reduce_sum.61 = bf16[512,512]{1,0:T(8,128)(2,1)} reduce(bf16[4,512,512]{2,1,0:T(8,128)(2,1)} %copy-done, bf16[]{:T(256)} %constant.34.clone.1), dimensions={0}, to_apply=%region_4.5 | reduce | flops 786432 | bytes 2621442 | tf_op jit(solution)/shard_map/reduce_sum | solution.py:243
  119.3 7.4 %collective-permute-done.4 = bf16[512,512]{1,0:T(8,128)(2,1)} collective-permute-done((bf16[512,512]{1,0:T(8,128)(2,1)}, bf16[512,512]{1,0:T(8,128)(2,1)}, u32[]{:S(2)}, u32[]{:S(2)}) %collective-permute-start.4) | collective-permute-done | bytes 524320 | tf_op jit(solution)/shard_map/ppermute | solution.py:220
  126.7 1.4 collective-permute-done.6
  128.0 11.0 %collective-permute-done.5 = bf16[512,512]{1,0:T(8,128)(2,1)} collective-permute-done((bf16[512,512]{1,0:T(8,128)(2,1)}, bf16[512,512]{1,0:T(8,128)(2,1)}, u32[]{:S(2)}, u32[]{:S(2)}) %collective-permute-start.5) | collective-permute-done | bytes 524320 | tf_op jit(solution)/shard_map/ppermute | solution.py:220
  139.1 1.7 %add_convert_fusion.2 = bf16[512,512]{1,0:T(8,128)(2,1)S(1)} fusion(bf16[512,512]{1,0:T(8,128)(2,1)} %collective-permute-done.6, bf16[512,512]{1,0:T(8,128)(2,1)} %collective-permute-done.5, bf16[512,512]{1,0:T(8,128)(2,1)} %collective-permute-done.4, bf16[2048,512]{1,0:T(8,128)(2,1)S(1)} %add_convert_fusion), kind=kLoop, calls=%fused_computation.9 | loop fusion | flops 2097152 | bytes 2621440 | tf_op jit(solution)/shard_map/convert_element_type | solution.py:247
  141.8 6.9 %all-to-all-start.3 = ((bf16[16,64,512]{2,1,0:T(8,128)(2,1)}), bf16[16,64,512]{2,1,0:T(8,128)(2,1)S(1)}, u32[]{:S(2)}, u32[]{:S(2)}) async-start(bf16[16,64,512]{2,1,0:T(8,128)(2,1)} %bitcast.7), calls=%async_computation.3 | async-start | bytes 2097152 | tf_op jit(solution)/shard_map/all_to_all | solution.py:261
  149.2 1.3 collective-permute-start.2
  150.5 2.0 %collective-permute-done.2 = bf16[576,128]{1,0:T(8,128)(2,1)S(1)} collective-permute-done((bf16[576,128]{1,0:T(8,128)(2,1)S(1)}, bf16[576,128]{1,0:T(8,128)(2,1)S(1)}, u32[]{:S(2)}, u32[]{:S(2)}) %collective-permute-start.2) | collective-permute-done | bytes 147488 | tf_op jit(solution)/shard_map/ppermute | solution.py:189
  153.2 11.7 %all-to-all-done.3 = bf16[16,64,512]{2,1,0:T(8,128)(2,1)S(1)} async-done(((bf16[16,64,512]{2,1,0:T(8,128)(2,1)}), bf16[16,64,512]{2,1,0:T(8,128)(2,1)S(1)}, u32[]{:S(2)}, u32[]{:S(2)}) %all-to-all-start.3) | async-done | bytes 1048608 | tf_op jit(solution)/shard_map/all_to_all | solution.py:261
  (30 shorter events, 9.9 us)
Async XLA Ops:
  0.6 12.9 %copy-start.3 = (s32[128]{0:T(128)S(1)}, s32[128]{0:T(128)}, u32[]{:S(2)}) copy-start(s32[128]{0:T(128)} %param.8) | copy-start | bytes 1540
  0.6 2.5 %collective-permute-start = (bf16[576,128]{1,0:T(8,128)(2,1)}, bf16[576,128]{1,0:T(8,128)(2,1)S(1)}, u32[]{:S(2)}, u32[]{:S(2)}) collective-permute-start(bf16[576,128]{1,0:T(8,128)(2,1)} %bitcast.19), channel_id=1, source_target_pairs={{0,8},{8,16},{16,24},{24,32},{32,40},{40,48},{48,56},{56,64},{64,7... | collective-permute-start | bytes 442376 | tf_op jit(solution)/shard_map/ppermute | solution.py:189
  5.2 24.3 %all-to-all-start = ((bf16[8,576,128]{2,1,0:T(8,128)(2,1)}), bf16[8,576,128]{2,1,0:T(8,128)(2,1)S(1)}, u32[]{:S(2)}, u32[]{:S(2)}) async-start(bf16[8,576,128]{2,1,0:T(8,128)(2,1)} %broadcast_select_fusion), calls=%async_computation | async-start | bytes 2359296 | tf_op jit(solution)/shard_map/all_to_all | solution.py:205
  29.6 1.0 copy-start.2
  57.9 6.3 %collective-permute-start.1 = (bf16[2048,512]{1,0:T(8,128)(2,1)}, bf16[2048,512]{1,0:T(8,128)(2,1)S(1)}, u32[]{:S(2)}, u32[]{:S(2)}) collective-permute-start(bf16[2048,512]{1,0:T(8,128)(2,1)} %get-tuple-element.23), channel_id=1, source_target_pairs={{0,8},{8,0},{16,24},{24,16},{32,40},{40,32},{48,56},{56,48},{64,72... | collective-permute-start | bytes 6291464 | tf_op jit(solution)/shard_map/ppermute | solution.py:225
  67.9 34.4 %all-to-all-start.1 = ((bf16[4,512,512]{2,1,0:T(8,128)(2,1)}), bf16[4,512,512]{2,1,0:T(8,128)(2,1)S(1)}, u32[]{:S(2)}, u32[]{:S(2)}) async-start(bf16[4,512,512]{2,1,0:T(8,128)(2,1)} %bitcast.5), calls=%async_computation.1 | async-start | bytes 4194304 | tf_op jit(solution)/shard_map/all_to_all | solution.py:235
  102.3 4.4 %copy-start = (bf16[4,512,512]{2,1,0:T(8,128)(2,1)}, bf16[4,512,512]{2,1,0:T(8,128)(2,1)S(1)}, u32[]{:S(2)}) copy-start(bf16[4,512,512]{2,1,0:T(8,128)(2,1)S(1)} %all-to-all-done.1) | copy-start | bytes 6291460
  102.3 4.6 %collective-permute-start.3 = (bf16[2048,512]{1,0:T(8,128)(2,1)}, bf16[2048,512]{1,0:T(8,128)(2,1)}, u32[]{:S(2)}, u32[]{:S(2)}) collective-permute-start(bf16[2048,512]{1,0:T(8,128)(2,1)} %get-tuple-element.39), channel_id=1, source_target_pairs={{0,8},{8,0},{16,24},{24,16},{32,40},{40,32},{48,56},{56,48},{64,72... | collective-permute-start | bytes 6291464 | tf_op jit(solution)/shard_map/ppermute | solution.py:225
  102.4 39.4 %all-to-all-start.2 = ((bf16[8,576,128]{2,1,0:T(8,128)(2,1)}), bf16[8,576,128]{2,1,0:T(8,128)(2,1)S(1)}, u32[]{:S(2)}, u32[]{:S(2)}) async-start(bf16[8,576,128]{2,1,0:T(8,128)(2,1)} %get-tuple-element.36), calls=%async_computation.2 | async-start | bytes 2359296 | tf_op jit(solution)/shard_map/all_to_all | solution.py:249
  110.9 15.8 %collective-permute-start.4 = (bf16[512,512]{1,0:T(8,128)(2,1)}, bf16[512,512]{1,0:T(8,128)(2,1)}, u32[]{:S(2)}, u32[]{:S(2)}) collective-permute-start(bf16[512,512]{1,0:T(8,128)(2,1)} %get-tuple-element.42), channel_id=1, source_target_pairs={{0,16},{8,24},{16,32},{24,40},{32,48},{40,56},{48,0},{56,8},{64,80... | collective-permute-start | bytes 1572872 | tf_op jit(solution)/shard_map/ppermute | solution.py:220
  112.9 15.1 %collective-permute-start.6 = (bf16[512,512]{1,0:T(8,128)(2,1)}, bf16[512,512]{1,0:T(8,128)(2,1)}, u32[]{:S(2)}, u32[]{:S(2)}) collective-permute-start(bf16[512,512]{1,0:T(8,128)(2,1)} %get-tuple-element.43), channel_id=1, source_target_pairs={{0,48},{8,56},{16,0},{24,8},{32,16},{40,24},{48,32},{56,40},{64,11... | collective-permute-start | bytes 1572872 | tf_op jit(solution)/shard_map/ppermute | solution.py:220
  114.1 24.9 %collective-permute-start.5 = (bf16[512,512]{1,0:T(8,128)(2,1)}, bf16[512,512]{1,0:T(8,128)(2,1)}, u32[]{:S(2)}, u32[]{:S(2)}) collective-permute-start(bf16[512,512]{1,0:T(8,128)(2,1)} %get-tuple-element.44), channel_id=1, source_target_pairs={{0,32},{8,40},{16,48},{24,56},{32,0},{40,8},{48,16},{56,24},{64,96... | collective-permute-start | bytes 1572872 | tf_op jit(solution)/shard_map/ppermute | solution.py:220
  119.3 21.5 %copy-start.1 = (bf16[512,512]{1,0:T(8,128)(2,1)S(1)}, bf16[512,512]{1,0:T(8,128)(2,1)}, u32[]{:S(2)}) copy-start(bf16[512,512]{1,0:T(8,128)(2,1)} %reduce_sum.61) | copy-start | bytes 1572868
  141.8 23.1 %all-to-all-start.3 = ((bf16[16,64,512]{2,1,0:T(8,128)(2,1)}), bf16[16,64,512]{2,1,0:T(8,128)(2,1)S(1)}, u32[]{:S(2)}, u32[]{:S(2)}) async-start(bf16[16,64,512]{2,1,0:T(8,128)(2,1)} %bitcast.7), calls=%async_computation.3 | async-start | bytes 2097152 | tf_op jit(solution)/shard_map/all_to_all | solution.py:261
  149.2 3.3 %collective-permute-start.2 = (bf16[576,128]{1,0:T(8,128)(2,1)S(1)}, bf16[576,128]{1,0:T(8,128)(2,1)S(1)}, u32[]{:S(2)}, u32[]{:S(2)}) collective-permute-start(bf16[576,128]{1,0:T(8,128)(2,1)S(1)} %get-tuple-element.40), channel_id=1, source_target_pairs={{8,0},{16,8},{24,16},{32,24},{40,32},{48,40},{56,48},{64,56},{72,6... | collective-permute-start | bytes 442376 | tf_op jit(solution)/shard_map/ppermute | solution.py:189

commit v2 on v1

--- a/solution.py
+++ b/solution.py
@@ -33,7 +33,47 @@
     return lax.dot_general(a, b, dims, preferred_element_type=F32)
 
 
-def attend_kernel(core_ref, keys_ref, bias_ref, q_ref, g_ref, w_ref, *rest, scale, is_first, is_last):
+def absorb_kernel(q_ref, g_ref, w_ref, qc_ref, ga_ref, *, scale):
+    tok = q_ref.shape[0]
+    for h in range(STEP_HEADS):
+        rows = slice(h * tok, (h + 1) * tok)
+        q_nope = q_ref[:, h * QDIM:h * QDIM + NOPE]
+        q_rope = q_ref[:, h * QDIM + NOPE:(h + 1) * QDIM]
+        key_weight = w_ref[:, h * KVDIM:h * KVDIM + NOPE]
+        value_weight = w_ref[:, h * KVDIM + NOPE:(h + 1) * KVDIM]
+        qc_ref[rows, :LATENT] = (dot_general(q_nope, key_weight, ROWS_ROWS) * scale).astype(BF16)
+        qc_ref[rows, LATENT:] = (q_rope.astype(F32) * scale).astype(BF16)
+        grad_head = g_ref[:, h * VDIM:(h + 1) * VDIM]
+        ga_ref[rows] = dot_general(grad_head, value_weight, ROWS_ROWS).astype(BF16)
+
+
+def absorb(queries, grad_out, kv_weight, scale):
+    tok = queries.shape[0]
+    rows = STEP_HEADS * tok
+    column = lambda s: (0, s)
+    row = lambda s: (s, 0)
+    return pl.pallas_call(
+        functools.partial(absorb_kernel, scale=scale),
+        grid=(HEADS // STEP_HEADS,),
+        in_specs=[
+            pl.BlockSpec((tok, STEP_HEADS * QDIM), column),
+            pl.BlockSpec((tok, STEP_HEADS * VDIM), column),
+            pl.BlockSpec((LATENT, STEP_HEADS * KVDIM), column),
+        ],
+        out_specs=[pl.BlockSpec((rows, WIDE), row), pl.BlockSpec((rows, LATENT), row)],
+        out_shape=[
+            jax.ShapeDtypeStruct((HEADS * tok, WIDE), BF16),
+            jax.ShapeDtypeStruct((HEADS * tok, LATENT), BF16),
+        ],
+        compiler_params=pltpu.CompilerParams(vmem_limit_bytes=24 * 1024 * 1024),
+        cost_estimate=pl.CostEstimate(
+            flops=6_000_000_000, bytes_accessed=20_000_000, transcendentals=0
+        ),
+        name="absorb",
+    )(queries, grad_out, kv_weight)
+
+
+def attend_kernel(core_ref, keys_ref, bias_ref, qc_ref, ga_ref, q_ref, g_ref, w_ref, *rest, scale, is_first, is_last):
     att_ref, gq_ref, keep_ref, send_ref, dkeys_ref, keys_t_ref, *acc = rest if is_first else rest[3:]
     acc_ref = acc[0] if is_last else dkeys_ref
     tok = q_ref.shape[0]
@@ -59,14 +99,8 @@
 
     keys_t = keys_t_ref[...]
     latent_t = keys_t_ref[:LATENT]
-    q_cat, g_abs = [], []
-    for h in range(STEP_HEADS):
-        qa = (dot_general(q_nope(h), key_weight(h), ROWS_ROWS) * scale).astype(BF16)
-        qr = (q_ref[:, h * QDIM + NOPE:(h + 1) * QDIM].astype(F32) * scale).astype(BF16)
-        q_cat.append(jnp.concatenate([qa, qr], axis=1))
-        g_abs.append(dot_general(grad_head(h), value_weight(h), ROWS_ROWS).astype(BF16))
-    q_cat = jnp.concatenate(q_cat, axis=0)
-    g_abs = jnp.concatenate(g_abs, axis=0)
+    q_cat = qc_ref[...]
+    g_abs = ga_ref[...]
     scores = dot(q_cat, keys_t)
     grad_probs = dot(g_abs, latent_t)
     bias = bias_ref[...]
@@ -121,13 +155,14 @@
                 dkeys_ref[s] = acc_ref[:, s * tok:(s + 1) * tok].astype(BF16)
 
 
-def attend_chunk(core, keys, bias, queries, grad_out, kv_weight, held, first, count, scale):
+def attend_chunk(core, keys, bias, absorbed, queries, grad_out, kv_weight, held, first, count, scale):
     tok = queries.shape[0]
     slots = keys.shape[0]
     n_keys = slots * tok
     is_first, is_last = first == 0, (first + count) * STEP_HEADS == HEADS
     whole = lambda s, c: (0, 0)
     column = lambda s, c: (0, first + s)
+    row = lambda s, c: (first + s, 0)
     block = lambda s, c: (lax.rem(s + count - c[1], count), 0)
     heads = count * STEP_HEADS
     parts_shape = jax.ShapeDtypeStruct((count * 2 * KVDIM, LATENT), BF16)
@@ -147,6 +182,8 @@
             in_specs=[
                 pl.BlockSpec(keys.shape, whole3),
                 pl.BlockSpec((tok, n_keys), whole),
+                pl.BlockSpec((STEP_HEADS * tok, WIDE), row),
+                pl.BlockSpec((STEP_HEADS * tok, LATENT), row),
                 pl.BlockSpec((tok, STEP_HEADS * QDIM), column),
                 pl.BlockSpec((tok, STEP_HEADS * VDIM), column),
                 pl.BlockSpec((LATENT, STEP_HEADS * KVDIM), column),
@@ -168,13 +205,13 @@
             parts_shape,
             jax.ShapeDtypeStruct(dkeys_shape, BF16 if is_last else F32),
         ],
-        input_output_aliases={7: 0, 8: 1} if held else {},
+        input_output_aliases={9: 0, 10: 1} if held else {},
         compiler_params=pltpu.CompilerParams(vmem_limit_bytes=56 * 1024 * 1024),
         cost_estimate=pl.CostEstimate(
             flops=heads * 1_000_000_000, bytes_accessed=heads * 1_000_000, transcendentals=0
         ),
         name="attend",
-    )(core, keys, bias, queries, grad_out, kv_weight, *held)
+    )(core, keys, bias, *absorbed, queries, grad_out, kv_weight, *held)
     return (dkeys, att, gq), keep, send
 
 
@@ -225,9 +262,10 @@
         other = lax.ppermute(send, "outer", swap)
         return (keep.astype(F32) + other.astype(F32)).astype(BF16)
 
+    absorbed = absorb(queries, grad_out, kv_weight, scale)
     which = jnp.stack([core, jnp.zeros_like(core)])
     held, keep, send = attend_chunk(
-        which, keys, bias, queries, grad_out, kv_weight, (), 0, 4, scale
+        which, keys, bias, absorbed, queries, grad_out, kv_weight, (), 0, 4, scale
     )
     pair = summed(keep, send)
     which, pair = lax.optimization_barrier((jnp.stack([core, row_y]), pair))
@@ -237,31 +275,39 @@
         axis_index_groups=same_xc, tiled=True,
     )
     held, keep, send = attend_chunk(
-        which, keys, bias, queries, grad_out, kv_weight, held, 4, 4, scale
+        which, keys, bias, absorbed, queries, grad_out, kv_weight, held, 4, 4, scale
     )
     held, keep, send, first = lax.optimization_barrier((held, keep, send, first))
-    first = jnp.sum(first.astype(F32), axis=0).astype(BF16)
     dkeys, attended, grad_query = held
-    pair = summed(keep, send).reshape(4, 512, LATENT)
-    second = sum(along_y(pair[by], by).astype(F32) for by in range(1, 4))
-    second = (second + pair[0].astype(F32)).astype(BF16)
-    reduced = [first, second]
-    arrived = lax.all_to_all(dkeys, "inner", split_axis=0, concat_axis=0, tiled=True).astype(F32)
+    other = lax.ppermute(send, "outer", swap)
+
+    def piece(by):
+        rows = slice(by * 512, (by + 1) * 512)
+        return (keep[rows].astype(F32) + other[rows].astype(F32)).astype(BF16)
+
+    moved = [along_y(piece(by), by) for by in (2, 1, 3)]
+    arrived = lax.all_to_all(dkeys, "inner", split_axis=0, concat_axis=0, tiled=True)
+    own_piece, first, arrived = lax.optimization_barrier((piece(0), first, arrived))
+    second = sum(m.astype(F32) for m in moved) + own_piece.astype(F32)
+
+    def along_inner(part):
+        part = part.astype(BF16).reshape(group, 64, LATENT)
+        part = lax.all_to_all(part, "inner", split_axis=0, concat_axis=0, tiled=True)
+        return jnp.sum(part.astype(F32), axis=0)
+
+    arrived = arrived.astype(F32)
     from_group = (slots >= inner)[:, None, None]
     own_term = jnp.sum(jnp.where(from_group, arrived, 0.0), axis=0)
     later_term = jnp.sum(jnp.where(from_group, 0.0, arrived), axis=0)
     next_term = shifted(later_term.astype(BF16), "outer", -1).astype(F32)
     grad_compressed = (own_term + next_term).astype(BF16).T
 
-    rest = [
-        [(x * 8 + y * 2 + c) * group + i for x in range(2) for i in range(group)]
-        for y in range(4) for c in range(2)
-    ]
-    reduced = jnp.concatenate(reduced, axis=0).reshape(16, 64, LATENT)
-    last = lax.all_to_all(
-        reduced, ("outer", "inner"), split_axis=0, concat_axis=0, axis_index_groups=rest, tiled=True
-    )
-    grad_weight_t = jnp.sum(last.astype(F32), axis=0)
+    first = along_inner(jnp.sum(first.astype(F32), axis=0))
+    second = along_inner(second)
+    low = outer < 8
+    crossing = jnp.where(low, second, first).astype(BF16)
+    crossing = lax.ppermute(crossing, "outer", [(o, o ^ 8) for o in range(n_outer)])
+    grad_weight_t = jnp.where(low, first, second) + crossing.astype(F32)
     return attended, grad_query, grad_compressed, grad_weight_t
 
 

time: 166 us -> 163 us (0.982)
  waiting for transfers between devices: 51.1 us -> 34.6 us
  local copies, waits for them, and re-layouts: 2.37 us -> 7.84 us
  starting transfers between devices: 36.5 us -> 40.1 us
  Pallas kernels: 55.2 us -> 58.6 us
    ppermute x3, waiting for transfers between devices: 19.8 us -> 8.58 us  [along_y(): lax.ppermute(shard, 'outer', [(o, o // 8 * 8 + (o % 8 + 2 * by) % 8) for...]
    all_to_all x1, waiting for transfers between devices: 13.5 us -> 3.82 us  [body(): lax.all_to_all(outgoing, 'inner', split_axis=0, concat_axis=0, tiled=True)]
    all_to_all x1, waiting for transfers between devices: 0.01 us -> 7.47 us  [body(): lax.all_to_all(dkeys, 'inner', split_axis=0, concat_axis=0, tiled=True)]
    unnamed x8 -> x10, local copies, waits for them, and re-layouts: 1.04 us -> 7.71 us
    convert_element_type x1 -> x3, other arithmetic: 1.67 us -> 6.63 us  [the longest x1 4 us: piece(): return (keep[rows].astype(F32) + other[rows].astype(F32)).astype(BF16)]
    all_to_all x1 -> x2, starting transfers between devices: 6.9 us -> 11.5 us  [along_inner(): lax.all_to_all(part, 'inner', split_axis=0, concat_axis=0, tiled=True)]
    pallas_call x0 -> x1, Pallas kernels: none -> 4.4 us  [absorb(): pl.pallas_call(functools.partial(absorb_kernel, scale=scale), grid=(HEADS...]
    convert_element_type x2 -> x1, other arithmetic: 6.48 us -> 3.49 us  [summed(): return (keep.astype(F32) + other.astype(F32)).astype(BF16)]
  transfers between devices with their start and end apart: 11 -> 13, of which waited for: 9 -> 7; matrix products, arithmetic and copies ran while one was open for 9% -> 9% of each run, Pallas kernels for 17% -> 20%
where the time goes in v2:
time: 163 us
  Pallas kernels  58.6 us (36%)
  starting transfers between devices  40.1 us (25%)
  waiting for transfers between devices  34.6 us (21%)
  other arithmetic  20.6 us (13%)
  local copies, waits for them, and re-layouts  7.84 us (5%)
    pallas_call x2, Pallas kernels, attend_chunk(): pl.pallas_call(functools.partial(attend_kernel, scale=scale, is_first=is_...  54.2 us
    all_to_all x2, starting transfers between devices, along_inner(): lax.all_to_all(part, 'inner', split_axis=0, concat_axis=0, tiled=True)  11.5 us
    all_to_all x2, waiting for transfers between devices, along_inner(): lax.all_to_all(part, 'inner', split_axis=0, concat_axis=0, tiled=True)  9.14 us
    ppermute x3, waiting for transfers between devices, along_y(): lax.ppermute(shard, 'outer', [(o, o // 8 * 8 + (o % 8 + 2 * by) % 8) for...  8.58 us
    all_to_all x1, starting transfers between devices, body(): lax.all_to_all(outgoing, 'inner', split_axis=0, concat_axis=0, tiled=True)  8.31 us
    unnamed x10, local copies, waits for them, and re-layouts  7.71 us
    all_to_all x1, waiting for transfers between devices, body(): lax.all_to_all(dkeys, 'inner', split_axis=0, concat_axis=0, tiled=True)  7.47 us
    all_to_all x1, starting transfers between devices, body(): lax.all_to_all(pair.reshape(4, 512, LATENT), 'outer', split_axis=0, conca...  5.8 us
  transfers between devices with their start and end apart: 13, of which 7 were waited for; matrix products, arithmetic and copies ran while one was open for 9% of the time, Pallas kernels for 20%

profile of v2, /device:TPU:0, one launch (start us, length us, event | category | flops | bytes accessed | tf_op | source)
XLA Modules:
  0.0 162.6 jit_solution(958273944653185185)
XLA Ops:
  0.6 1.3 collective-permute-start
  4.8 2.2 %broadcast_select_fusion = bf16[8,576,128]{2,1,0:T(8,128)(2,1)} fusion(pred[8]{0:T(512)(128)(4,1)S(1)} %iota_compare_fusion.3, bf16[576,128]{1,0:T(8,128)(2,1)S(1)} %collective-permute-done, bf16[576,128]{1,0:T(8,128)(2,1)} %bitcast.22), kind=kLoop, calls=%fused_computation.5 | loop fusion | flops 589824 | bytes 1474568 | tf_op jit(solution)/shard_map/jit(_where)/select_n | solution.py:241
  7.1 8.3 %all-to-all-start = ((bf16[8,576,128]{2,1,0:T(8,128)(2,1)}), bf16[8,576,128]{2,1,0:T(8,128)(2,1)}, u32[]{:S(2)}, u32[]{:S(2)}) async-start(bf16[8,576,128]{2,1,0:T(8,128)(2,1)} %broadcast_select_fusion), calls=%async_computation | async-start | bytes 2359296 | tf_op jit(solution)/shard_map/all_to_all | solution.py:242
  17.0 3.4 %copy-done = bf16[512,8192]{1,0:T(8,128)(2,1)S(1)} copy-done((bf16[512,8192]{1,0:T(8,128)(2,1)S(1)}, bf16[512,8192]{1,0:T(8,128)(2,1)}, u32[]{:S(2)}) %copy-start) | copy-done | bytes 8388632
  20.4 4.4 %absorb.1 = (bf16[4096,576]{1,0:T(8,128)(2,1)S(1)}, bf16[4096,512]{1,0:T(8,128)(2,1)S(1)}) custom-call(bf16[128,6144]{1,0:T(8,128)(2,1)S(1)} %copy-done.1, bf16[128,4096]{1,0:T(8,128)(2,1)S(1)} %copy-done.2, bf16[512,8192]{1,0:T(8,128)(2,1)S(1)} %copy-done), custom_call_target="tpu_custom_call" | custom-call | flops 6000000000 | bytes 20000000 | tf_op jit(solution)/shard_map/absorb/pallas_call | solution.py:55
  24.8 2.3 %copy-done.3 = bf16[4096,576]{1,0:T(8,128)(2,1)} copy-done((bf16[4096,576]{1,0:T(8,128)(2,1)}, bf16[4096,576]{1,0:T(8,128)(2,1)S(1)}, u32[]{:S(2)}) %copy-start.3) | copy-done | bytes 4718616
  27.1 2.0 %copy-done.4 = bf16[4096,512]{1,0:T(8,128)(2,1)} copy-done((bf16[4096,512]{1,0:T(8,128)(2,1)}, bf16[4096,512]{1,0:T(8,128)(2,1)S(1)}, u32[]{:S(2)}) %copy-start.4) | copy-done | bytes 4194328
  29.1 3.8 %all-to-all-done.keys_ref = bf16[8,576,128]{2,1,0:T(8,128)(2,1)} async-done(((bf16[8,576,128]{2,1,0:T(8,128)(2,1)}), bf16[8,576,128]{2,1,0:T(8,128)(2,1)}, u32[]{:S(2)}, u32[]{:S(2)}) %all-to-all-start) | async-done | bytes 1179680 | tf_op jit(solution)/shard_map/all_to_all | solution.py:242
  32.9 26.8 %attend.2 = (bf16[128,4096]{1,0:T(8,128)(2,1)}, bf16[128,6144]{1,0:T(8,128)(2,1)}, bf16[2048,512]{1,0:T(8,128)(2,1)}, bf16[2048,512]{1,0:T(8,128)(2,1)}, f32[576,1024]{1,0:T(8,128)}) custom-call(s32[2]{0:T(128)} %pad_add_fusion.1.core_ref, bf16[8,576,128]{2,1,0:T(8,128)(2,1)} %all-to-all-done.keys_ref, f32[128,1024]{1,0:T(8,128)} %fusion.3.bias_ref, ...), custom_call_target="tpu_custom_call" | custom-call | flops 16000000000 | bytes 16000000 | tf_op jit(solution)/shard_map/attend/pallas_call | solution.py:177
  60.8 3.3 %collective-permute-done.1 = bf16[2048,512]{1,0:T(8,128)(2,1)S(1)} collective-permute-done((bf16[2048,512]{1,0:T(8,128)(2,1)}, bf16[2048,512]{1,0:T(8,128)(2,1)S(1)}, u32[]{:S(2)}, u32[]{:S(2)}) %collective-permute-start.1) | collective-permute-done | bytes 2097184 | tf_op jit(solution)/shard_map/ppermute | solution.py:262
  64.2 3.5 %add_convert_fusion = bf16[2048,512]{1,0:T(8,128)(2,1)} fusion(bf16[2048,512]{1,0:T(8,128)(2,1)S(1)} %collective-permute-done.1, bf16[2048,512]{1,0:T(8,128)(2,1)} %get-tuple-element.29), kind=kLoop, calls=%fused_computation | loop fusion | flops 4194304 | bytes 6291456 | tf_op jit(solution)/shard_map/convert_element_type | solution.py:263
  67.7 5.8 %all-to-all-start.1 = ((bf16[4,512,512]{2,1,0:T(8,128)(2,1)}), bf16[4,512,512]{2,1,0:T(8,128)(2,1)S(1)}, u32[]{:S(2)}, u32[]{:S(2)}) async-start(bf16[4,512,512]{2,1,0:T(8,128)(2,1)} %bitcast.5), calls=%async_computation.1 | async-start | bytes 4194304 | tf_op jit(solution)/shard_map/all_to_all | solution.py:273
  73.5 27.4 %attend.3 = (bf16[128,4096]{1,0:T(8,128)(2,1)}, bf16[128,6144]{1,0:T(8,128)(2,1)}, bf16[2048,512]{1,0:T(8,128)(2,1)}, bf16[2048,512]{1,0:T(8,128)(2,1)}, bf16[8,576,128]{2,1,0:T(8,128)(2,1)}) custom-call(s32[2]{0:T(128)} %pad_add_fusion.core_ref, bf16[8,576,128]{2,1,0:T(8,128)(2,1)} %all-to-all-done.keys_ref, ...), custom_call_target="tpu_custom_call", output_to_operand_aliasing={{0}: (9, {}), {1}: (10, {})} | custom-call | flops 16000000000 | bytes 16000000 | tf_op jit(solution)/shard_map/attend/pallas_call | solution.py:177
  101.0 4.3 %all-to-all-start.2 = ((bf16[8,576,128]{2,1,0:T(8,128)(2,1)}), bf16[8,576,128]{2,1,0:T(8,128)(2,1)S(1)}, u32[]{:S(2)}, u32[]{:S(2)}) async-start(bf16[8,576,128]{2,1,0:T(8,128)(2,1)} %get-tuple-element.46), calls=%async_computation.2 | async-start | bytes 2359296 | tf_op jit(solution)/shard_map/all_to_all | solution.py:289
  105.5 4.0 %add_convert_fusion.4 = (bf16[512,512]{1,0:T(8,128)(2,1)}, bf16[512,512]{1,0:T(8,128)(2,1)}, bf16[512,512]{1,0:T(8,128)(2,1)}, bf16[512,512]{1,0:T(8,128)(2,1)}) fusion(bf16[2048,512]{1,0:T(8,128)(2,1)} %collective-permute-done.2, bf16[2048,512]{1,0:T(8,128)(2,1)} %get-tuple-element.43), kind=kLoop, calls=%fused_computation.10 | loop fusion | flops 4194304 | bytes 6291456 | tf_op jit(solution)/shard_map/convert_element_type | solution.py:286
  109.5 3.5 %collective-permute-start.4 = (bf16[512,512]{1,0:T(8,128)(2,1)}, bf16[512,512]{1,0:T(8,128)(2,1)}, u32[]{:S(2)}, u32[]{:S(2)}) collective-permute-start(bf16[512,512]{1,0:T(8,128)(2,1)} %get-tuple-element.52), channel_id=1, source_target_pairs={{0,32},{8,40},{16,48},{24,56},{32,0},{40,8},{48,16},{56,24},{64,96... | collective-permute-start | bytes 1572872 | tf_op jit(solution)/shard_map/ppermute | solution.py:257
  115.0 7.5 %all-to-all-done.2 = bf16[8,576,128]{2,1,0:T(8,128)(2,1)S(1)} async-done(((bf16[8,576,128]{2,1,0:T(8,128)(2,1)}), bf16[8,576,128]{2,1,0:T(8,128)(2,1)S(1)}, u32[]{:S(2)}, u32[]{:S(2)}) %all-to-all-start.2) | async-done | bytes 1179680 | tf_op jit(solution)/shard_map/all_to_all | solution.py:289
  123.7 4.8 %all-to-all-start.3 = ((bf16[8,64,512]{2,1,0:T(8,128)(2,1)}), bf16[8,64,512]{2,1,0:T(8,128)(2,1)S(1)}, u32[]{:S(2)}, u32[]{:S(2)}) async-start(bf16[8,64,512]{2,1,0:T(8,128)(2,1)} %bitcast.19), calls=%async_computation.3 | async-start | bytes 1048576 | tf_op jit(solution)/shard_map/all_to_all | solution.py:295
  128.5 8.6 %collective-permute-done.6 = bf16[512,512]{1,0:T(8,128)(2,1)} collective-permute-done((bf16[512,512]{1,0:T(8,128)(2,1)}, bf16[512,512]{1,0:T(8,128)(2,1)}, u32[]{:S(2)}, u32[]{:S(2)}) %collective-permute-start.6) | collective-permute-done | bytes 524320 | tf_op jit(solution)/shard_map/ppermute | solution.py:257
  137.1 2.6 %add_convert_fusion.1 = bf16[512,512]{1,0:T(8,128)(2,1)} fusion(bf16[512,512]{1,0:T(8,128)(2,1)} %get-tuple-element.49, bf16[512,512]{1,0:T(8,128)(2,1)} %collective-permute-done.6, bf16[512,512]{1,0:T(8,128)(2,1)} %collective-permute-done.5, bf16[512,512]{1,0:T(8,128)(2,1)} %collective-permute-done.4), kind=kLoop, calls=%fused_computation.7 | loop fusion | flops 2097152 | bytes 2621440 | tf_op jit(solution)/shard_map/convert_element_type | solution.py:294
  139.7 6.8 %all-to-all-start.4 = ((bf16[8,64,512]{2,1,0:T(8,128)(2,1)}), bf16[8,64,512]{2,1,0:T(8,128)(2,1)S(1)}, u32[]{:S(2)}, u32[]{:S(2)}) async-start(bf16[8,64,512]{2,1,0:T(8,128)(2,1)} %bitcast.8), calls=%async_computation.4 | async-start | bytes 1048576 | tf_op jit(solution)/shard_map/all_to_all | solution.py:295
  148.4 9.1 %all-to-all-done.4 = bf16[8,64,512]{2,1,0:T(8,128)(2,1)S(1)} async-done(((bf16[8,64,512]{2,1,0:T(8,128)(2,1)}), bf16[8,64,512]{2,1,0:T(8,128)(2,1)S(1)}, u32[]{:S(2)}, u32[]{:S(2)}) %all-to-all-start.4) | async-done | bytes 524320 | tf_op jit(solution)/shard_map/all_to_all | solution.py:295
  157.6 1.6 collective-permute-start.7
  159.8 2.1 %collective-permute-done.7 = bf16[64,512]{1,0:T(8,128)(2,1)S(1)} collective-permute-done((bf16[64,512]{1,0:T(8,128)(2,1)S(1)}, bf16[64,512]{1,0:T(8,128)(2,1)S(1)}, u32[]{:S(2)}, u32[]{:S(2)}) %collective-permute-start.7) | collective-permute-done | bytes 65568 | tf_op jit(solution)/shard_map/ppermute | solution.py:309
  (38 shorter events, 12.4 us)
Async XLA Ops:
  0.6 4.2 %collective-permute-start = (bf16[576,128]{1,0:T(8,128)(2,1)}, bf16[576,128]{1,0:T(8,128)(2,1)S(1)}, u32[]{:S(2)}, u32[]{:S(2)}) collective-permute-start(bf16[576,128]{1,0:T(8,128)(2,1)} %bitcast.21), channel_id=1, source_target_pairs={{0,8},{8,16},{16,24},{24,32},{32,40},{40,48},{48,56},{56,64},{64,7... | collective-permute-start | bytes 442376 | tf_op jit(solution)/shard_map/ppermute | solution.py:226
  4.8 12.2 %copy-start.1 = (bf16[128,6144]{1,0:T(8,128)(2,1)S(1)}, bf16[128,6144]{1,0:T(8,128)(2,1)}, u32[]{:S(2)}) copy-start(bf16[128,6144]{1,0:T(8,128)(2,1)} %q_ref.5) | copy-start | bytes 4718596
  4.8 12.2 %copy-start.2 = (bf16[128,4096]{1,0:T(8,128)(2,1)S(1)}, bf16[128,4096]{1,0:T(8,128)(2,1)}, u32[]{:S(2)}) copy-start(bf16[128,4096]{1,0:T(8,128)(2,1)} %g_ref.5) | copy-start | bytes 3145732
  7.1 25.9 %all-to-all-start = ((bf16[8,576,128]{2,1,0:T(8,128)(2,1)}), bf16[8,576,128]{2,1,0:T(8,128)(2,1)}, u32[]{:S(2)}, u32[]{:S(2)}) async-start(bf16[8,576,128]{2,1,0:T(8,128)(2,1)} %broadcast_select_fusion), calls=%async_computation | async-start | bytes 2359296 | tf_op jit(solution)/shard_map/all_to_all | solution.py:242
  17.0 3.4 %copy-start = (bf16[512,8192]{1,0:T(8,128)(2,1)S(1)}, bf16[512,8192]{1,0:T(8,128)(2,1)}, u32[]{:S(2)}) copy-start(bf16[512,8192]{1,0:T(8,128)(2,1)} %w_ref.5) | copy-start | bytes 25165828
  24.8 2.3 %copy-start.3 = (bf16[4096,576]{1,0:T(8,128)(2,1)}, bf16[4096,576]{1,0:T(8,128)(2,1)S(1)}, u32[]{:S(2)}) copy-start(bf16[4096,576]{1,0:T(8,128)(2,1)S(1)} %get-tuple-element.27.qc_ref) | copy-start | bytes 14155780
  27.1 2.0 %copy-start.4 = (bf16[4096,512]{1,0:T(8,128)(2,1)}, bf16[4096,512]{1,0:T(8,128)(2,1)S(1)}, u32[]{:S(2)}) copy-start(bf16[4096,512]{1,0:T(8,128)(2,1)S(1)} %get-tuple-element.28.ga_ref) | copy-start | bytes 12582916
  59.8 4.4 %collective-permute-start.1 = (bf16[2048,512]{1,0:T(8,128)(2,1)}, bf16[2048,512]{1,0:T(8,128)(2,1)S(1)}, u32[]{:S(2)}, u32[]{:S(2)}) collective-permute-start(bf16[2048,512]{1,0:T(8,128)(2,1)} %get-tuple-element.30), channel_id=1, source_target_pairs={{0,8},{8,0},{16,24},{24,16},{32,40},{40,32},{48,56},{56,48},{64,72... | collective-permute-start | bytes 6291464 | tf_op jit(solution)/shard_map/ppermute | solution.py:262
  67.7 33.2 %all-to-all-start.1 = ((bf16[4,512,512]{2,1,0:T(8,128)(2,1)}), bf16[4,512,512]{2,1,0:T(8,128)(2,1)S(1)}, u32[]{:S(2)}, u32[]{:S(2)}) async-start(bf16[4,512,512]{2,1,0:T(8,128)(2,1)} %bitcast.5), calls=%async_computation.1 | async-start | bytes 4194304 | tf_op jit(solution)/shard_map/all_to_all | solution.py:273
  100.9 4.6 %collective-permute-start.2 = (bf16[2048,512]{1,0:T(8,128)(2,1)}, bf16[2048,512]{1,0:T(8,128)(2,1)}, u32[]{:S(2)}, u32[]{:S(2)}) collective-permute-start(bf16[2048,512]{1,0:T(8,128)(2,1)} %get-tuple-element.44), channel_id=1, source_target_pairs={{0,8},{8,0},{16,24},{24,16},{32,40},{40,32},{48,56},{56,48},{64,72... | collective-permute-start | bytes 6291464 | tf_op jit(solution)/shard_map/ppermute | solution.py:282
  101.0 21.5 %all-to-all-start.2 = ((bf16[8,576,128]{2,1,0:T(8,128)(2,1)}), bf16[8,576,128]{2,1,0:T(8,128)(2,1)S(1)}, u32[]{:S(2)}, u32[]{:S(2)}) async-start(bf16[8,576,128]{2,1,0:T(8,128)(2,1)} %get-tuple-element.46), calls=%async_computation.2 | async-start | bytes 2359296 | tf_op jit(solution)/shard_map/all_to_all | solution.py:289
  109.5 19.0 %collective-permute-start.4 = (bf16[512,512]{1,0:T(8,128)(2,1)}, bf16[512,512]{1,0:T(8,128)(2,1)}, u32[]{:S(2)}, u32[]{:S(2)}) collective-permute-start(bf16[512,512]{1,0:T(8,128)(2,1)} %get-tuple-element.52), channel_id=1, source_target_pairs={{0,32},{8,40},{16,48},{24,56},{32,0},{40,8},{48,16},{56,24},{64,96... | collective-permute-start | bytes 1572872 | tf_op jit(solution)/shard_map/ppermute | solution.py:257
  113.0 24.1 %collective-permute-start.6 = (bf16[512,512]{1,0:T(8,128)(2,1)}, bf16[512,512]{1,0:T(8,128)(2,1)}, u32[]{:S(2)}, u32[]{:S(2)}) collective-permute-start(bf16[512,512]{1,0:T(8,128)(2,1)} %get-tuple-element.53), channel_id=1, source_target_pairs={{0,48},{8,56},{16,0},{24,8},{32,16},{40,24},{48,32},{56,40},{64,11... | collective-permute-start | bytes 1572872 | tf_op jit(solution)/shard_map/ppermute | solution.py:257
  114.1 22.9 %collective-permute-start.5 = (bf16[512,512]{1,0:T(8,128)(2,1)}, bf16[512,512]{1,0:T(8,128)(2,1)}, u32[]{:S(2)}, u32[]{:S(2)}) collective-permute-start(bf16[512,512]{1,0:T(8,128)(2,1)} %get-tuple-element.54), channel_id=1, source_target_pairs={{0,16},{8,24},{16,32},{24,40},{32,48},{40,56},{48,0},{56,8},{64,80... | collective-permute-start | bytes 1572872 | tf_op jit(solution)/shard_map/ppermute | solution.py:257
  123.7 16.0 %all-to-all-start.3 = ((bf16[8,64,512]{2,1,0:T(8,128)(2,1)}), bf16[8,64,512]{2,1,0:T(8,128)(2,1)S(1)}, u32[]{:S(2)}, u32[]{:S(2)}) async-start(bf16[8,64,512]{2,1,0:T(8,128)(2,1)} %bitcast.19), calls=%async_computation.3 | async-start | bytes 1048576 | tf_op jit(solution)/shard_map/all_to_all | solution.py:295
  139.7 17.8 %all-to-all-start.4 = ((bf16[8,64,512]{2,1,0:T(8,128)(2,1)}), bf16[8,64,512]{2,1,0:T(8,128)(2,1)S(1)}, u32[]{:S(2)}, u32[]{:S(2)}) async-start(bf16[8,64,512]{2,1,0:T(8,128)(2,1)} %bitcast.8), calls=%async_computation.4 | async-start | bytes 1048576 | tf_op jit(solution)/shard_map/all_to_all | solution.py:295
  147.0 12.2 %collective-permute-start.3 = (bf16[576,128]{1,0:T(8,128)(2,1)S(1)}, bf16[576,128]{1,0:T(8,128)(2,1)S(1)}, u32[]{:S(2)}, u32[]{:S(2)}) collective-permute-start(bf16[576,128]{1,0:T(8,128)(2,1)S(1)} %get-tuple-element.50), channel_id=1, source_target_pairs={{8,0},{16,8},{24,16},{32,24},{40,32},{48,40},{56,48},{64,56},{72,6... | collective-permute-start | bytes 442376 | tf_op jit(solution)/shard_map/ppermute | solution.py:226
  157.6 4.3 %collective-permute-start.7 = (bf16[64,512]{1,0:T(8,128)(2,1)S(1)}, bf16[64,512]{1,0:T(8,128)(2,1)S(1)}, u32[]{:S(2)}, u32[]{:S(2)}) collective-permute-start(bf16[64,512]{1,0:T(8,128)(2,1)S(1)} %select_convert_fusion), channel_id=1, source_target_pairs={{0,64},{8,72},{16,80},{24,88},{32,96},{40,104},{48,112},{56,120},{... | collective-permute-start | bytes 196616 | tf_op jit(solution)/shard_map/ppermute | solution.py:309

commit v3 on v2

--- a/solution.py
+++ b/solution.py
@@ -170,7 +170,7 @@
     dkeys_shape = keys.shape if is_last else (WIDE, n_keys)
     whole3 = lambda s, c: (0, 0, 0)
     held_specs = [
-        pl.BlockSpec((WIDE, n_keys), whole),
+        pl.BlockSpec(memory_space=pltpu.VMEM),
         pl.BlockSpec(memory_space=pl.ANY),
         pl.BlockSpec(memory_space=pl.ANY),
     ]
@@ -180,8 +180,8 @@
             num_scalar_prefetch=1,
             grid=(count,),
             in_specs=[
-                pl.BlockSpec(keys.shape, whole3),
-                pl.BlockSpec((tok, n_keys), whole),
+                pl.BlockSpec(memory_space=pltpu.VMEM),
+                pl.BlockSpec(memory_space=pltpu.VMEM),
                 pl.BlockSpec((STEP_HEADS * tok, WIDE), row),
                 pl.BlockSpec((STEP_HEADS * tok, LATENT), row),
                 pl.BlockSpec((tok, STEP_HEADS * QDIM), column),
@@ -193,7 +193,7 @@
                 pl.BlockSpec((tok, STEP_HEADS * QDIM), column),
                 parts_spec,
                 parts_spec,
-                pl.BlockSpec(dkeys_shape, whole3 if is_last else whole),
+                pl.BlockSpec(memory_space=pltpu.VMEM),
             ],
             scratch_shapes=[pltpu.VMEM((WIDE, n_keys), BF16)]
             + [pltpu.VMEM((WIDE, n_keys), F32)] * is_last,
@@ -206,7 +206,7 @@
             jax.ShapeDtypeStruct(dkeys_shape, BF16 if is_last else F32),
         ],
         input_output_aliases={9: 0, 10: 1} if held else {},
-        compiler_params=pltpu.CompilerParams(vmem_limit_bytes=56 * 1024 * 1024),
+        compiler_params=pltpu.CompilerParams(vmem_limit_bytes=52 * 1024 * 1024),
         cost_estimate=pl.CostEstimate(
             flops=heads * 1_000_000_000, bytes_accessed=heads * 1_000_000, transcendentals=0
         ),

time: 163 us -> 162 us (level)
  waiting for transfers between devices: 34.6 us -> 38.7 us
  starting transfers between devices: 40.1 us -> 36.5 us
    all_to_all x2, waiting for transfers between devices: 9.14 us -> 12.2 us  [along_inner(): lax.all_to_all(part, 'inner', split_axis=0, concat_axis=0, tiled=True)]
    all_to_all x2, starting transfers between devices: 11.5 us -> 8.54 us  [along_inner(): lax.all_to_all(part, 'inner', split_axis=0, concat_axis=0, tiled=True)]
    ppermute x3, waiting for transfers between devices: 8.58 us -> 5.93 us  [along_y(): lax.ppermute(shard, 'outer', [(o, o // 8 * 8 + (o % 8 + 2 * by) % 8) for...]
    unnamed x10 -> x14, local copies, waits for them, and re-layouts: 7.71 us -> 7.71 us
  transfers between devices with their start and end apart: 13 -> 13, of which waited for: 7 -> 9; matrix products, arithmetic and copies ran while one was open for 9% -> 8% of each run, Pallas kernels for 20% -> 19%
where the time goes in v3:
time: 162 us; the launch traced here: 161 us
  Pallas kernels  57.5 us (35%)
  waiting for transfers between devices  38.7 us (24%)
  starting transfers between devices  36.5 us (23%)
  other arithmetic  19.7 us (12%)
  local copies, waits for them, and re-layouts  7.85 us (5%)
    pallas_call x2, Pallas kernels, attend_chunk(): pl.pallas_call(functools.partial(attend_kernel, scale=scale, is_first=is_...  53.1 us
    all_to_all x2, waiting for transfers between devices, along_inner(): lax.all_to_all(part, 'inner', split_axis=0, concat_axis=0, tiled=True)  12.2 us
    all_to_all x2, starting transfers between devices, along_inner(): lax.all_to_all(part, 'inner', split_axis=0, concat_axis=0, tiled=True)  8.54 us
    all_to_all x1, waiting for transfers between devices, body(): lax.all_to_all(dkeys, 'inner', split_axis=0, concat_axis=0, tiled=True)  8.43 us
    all_to_all x1, starting transfers between devices, body(): lax.all_to_all(outgoing, 'inner', split_axis=0, concat_axis=0, tiled=True)  8.31 us
    unnamed x14, local copies, waits for them, and re-layouts  7.71 us
    ppermute x3, waiting for transfers between devices, along_y(): lax.ppermute(shard, 'outer', [(o, o // 8 * 8 + (o % 8 + 2 * by) % 8) for...  5.93 us
    all_to_all x1, starting transfers between devices, body(): lax.all_to_all(pair.reshape(4, 512, LATENT), 'outer', split_axis=0, conca...  5.8 us
  transfers between devices with their start and end apart: 13, of which 9 were waited for; matrix products, arithmetic and copies ran while one was open for 8% of the time, Pallas kernels for 19%

profile of v3, /device:TPU:0, one launch (start us, length us, event | category | flops | bytes accessed | tf_op | source)
XLA Modules:
  0.0 161.0 jit_solution(4642062054218885844)
XLA Ops:
  4.8 2.2 %broadcast_select_fusion = bf16[8,576,128]{2,1,0:T(8,128)(2,1)} fusion(pred[8]{0:T(512)(128)(4,1)S(1)} %iota_compare_fusion.3, bf16[576,128]{1,0:T(8,128)(2,1)S(1)} %collective-permute-done, bf16[576,128]{1,0:T(8,128)(2,1)} %bitcast.22), kind=kLoop, calls=%fused_computation.5 | loop fusion | flops 589824 | bytes 1474568 | tf_op jit(solution)/shard_map/jit(_where)/select_n | solution.py:241
  7.1 8.3 %all-to-all-start = ((bf16[8,576,128]{2,1,0:T(8,128)(2,1)}), bf16[8,576,128]{2,1,0:T(8,128)(2,1)}, u32[]{:S(2)}, u32[]{:S(2)}) async-start(bf16[8,576,128]{2,1,0:T(8,128)(2,1)} %broadcast_select_fusion), calls=%async_computation | async-start | bytes 2359296 | tf_op jit(solution)/shard_map/all_to_all | solution.py:242
  15.7 3.4 %copy-done = bf16[512,8192]{1,0:T(8,128)(2,1)S(1)} copy-done((bf16[512,8192]{1,0:T(8,128)(2,1)S(1)}, bf16[512,8192]{1,0:T(8,128)(2,1)}, u32[]{:S(2)}) %copy-start) | copy-done | bytes 8388632
  19.1 4.4 %absorb.1 = (bf16[4096,576]{1,0:T(8,128)(2,1)S(1)}, bf16[4096,512]{1,0:T(8,128)(2,1)S(1)}) custom-call(bf16[128,6144]{1,0:T(8,128)(2,1)S(1)} %copy-done.1, bf16[128,4096]{1,0:T(8,128)(2,1)S(1)} %copy-done.2, bf16[512,8192]{1,0:T(8,128)(2,1)S(1)} %copy-done), custom_call_target="tpu_custom_call" | custom-call | flops 6000000000 | bytes 20000000 | tf_op jit(solution)/shard_map/absorb/pallas_call | solution.py:55
  23.5 2.3 %copy-done.3 = bf16[4096,576]{1,0:T(8,128)(2,1)} copy-done((bf16[4096,576]{1,0:T(8,128)(2,1)}, bf16[4096,576]{1,0:T(8,128)(2,1)S(1)}, u32[]{:S(2)}) %copy-start.3) | copy-done | bytes 4718616
  25.8 2.0 %copy-done.4 = bf16[4096,512]{1,0:T(8,128)(2,1)} copy-done((bf16[4096,512]{1,0:T(8,128)(2,1)}, bf16[4096,512]{1,0:T(8,128)(2,1)S(1)}, u32[]{:S(2)}) %copy-start.4) | copy-done | bytes 4194328
  27.8 5.1 %all-to-all-done.keys_ref = bf16[8,576,128]{2,1,0:T(8,128)(2,1)} async-done(((bf16[8,576,128]{2,1,0:T(8,128)(2,1)}), bf16[8,576,128]{2,1,0:T(8,128)(2,1)}, u32[]{:S(2)}, u32[]{:S(2)}) %all-to-all-start) | async-done | bytes 1179680 | tf_op jit(solution)/shard_map/all_to_all | solution.py:242
  32.9 26.3 %attend.2 = (bf16[128,4096]{1,0:T(8,128)(2,1)}, bf16[128,6144]{1,0:T(8,128)(2,1)}, bf16[2048,512]{1,0:T(8,128)(2,1)}, bf16[2048,512]{1,0:T(8,128)(2,1)}, f32[576,1024]{1,0:T(8,128)}) custom-call(s32[2]{0:T(128)S(1)} %pad_add_fusion.1.core_ref, bf16[8,576,128]{2,1,0:T(8,128)(2,1)} %all-to-all-done.keys_ref, f32[128,1024]{1,0:T(8,128)S(1)} %fusion.3.bias_ref, ...), custom_call_target="tpu_custom_call" | custom-call | flops 16000000000 | bytes 16000000 | tf_op jit(solution)/shard_map/attend/pallas_call | solution.py:177
  59.7 4.1 %collective-permute-done.1 = bf16[2048,512]{1,0:T(8,128)(2,1)} collective-permute-done((bf16[2048,512]{1,0:T(8,128)(2,1)}, bf16[2048,512]{1,0:T(8,128)(2,1)}, u32[]{:S(2)}, u32[]{:S(2)}) %collective-permute-start.1) | collective-permute-done | bytes 2097184 | tf_op jit(solution)/shard_map/ppermute | solution.py:262
  63.7 4.2 %add_convert_fusion = bf16[2048,512]{1,0:T(8,128)(2,1)} fusion(bf16[2048,512]{1,0:T(8,128)(2,1)} %collective-permute-done.1, bf16[2048,512]{1,0:T(8,128)(2,1)} %get-tuple-element.29), kind=kLoop, calls=%fused_computation | loop fusion | flops 4194304 | bytes 6291456 | tf_op jit(solution)/shard_map/convert_element_type | solution.py:263
  67.9 5.8 %all-to-all-start.1 = ((bf16[4,512,512]{2,1,0:T(8,128)(2,1)}), bf16[4,512,512]{2,1,0:T(8,128)(2,1)}, u32[]{:S(2)}, u32[]{:S(2)}) async-start(bf16[4,512,512]{2,1,0:T(8,128)(2,1)} %bitcast.19), calls=%async_computation.1 | async-start | bytes 4194304 | tf_op jit(solution)/shard_map/all_to_all | solution.py:273
  73.7 26.8 %attend.3 = (bf16[128,4096]{1,0:T(8,128)(2,1)}, bf16[128,6144]{1,0:T(8,128)(2,1)}, bf16[2048,512]{1,0:T(8,128)(2,1)}, bf16[2048,512]{1,0:T(8,128)(2,1)}, bf16[8,576,128]{2,1,0:T(8,128)(2,1)}) custom-call(s32[2]{0:T(128)S(1)} %pad_add_fusion.core_ref, bf16[8,576,128]{2,1,0:T(8,128)(2,1)} %all-to-all-done.keys_ref, ...), custom_call_target="tpu_custom_call", output_to_operand_aliasing={{0}: (9, {}), {1}: (10, {})} | custom-call | flops 16000000000 | bytes 16000000 | tf_op jit(solution)/shard_map/attend/pallas_call | solution.py:177
  100.8 4.4 %all-to-all-start.2 = ((bf16[8,576,128]{2,1,0:T(8,128)(2,1)}), bf16[8,576,128]{2,1,0:T(8,128)(2,1)S(1)}, u32[]{:S(2)}, u32[]{:S(2)}) async-start(bf16[8,576,128]{2,1,0:T(8,128)(2,1)} %get-tuple-element.46), calls=%async_computation.2 | async-start | bytes 2359296 | tf_op jit(solution)/shard_map/all_to_all | solution.py:289
  105.3 3.3 %add_convert_fusion.4 = (bf16[512,512]{1,0:T(8,128)(2,1)}, bf16[512,512]{1,0:T(8,128)(2,1)}, bf16[512,512]{1,0:T(8,128)(2,1)}, bf16[512,512]{1,0:T(8,128)(2,1)}) fusion(bf16[2048,512]{1,0:T(8,128)(2,1)} %collective-permute-done.2, bf16[2048,512]{1,0:T(8,128)(2,1)S(1)} %copy-done.5), kind=kLoop, calls=%fused_computation.10 | loop fusion | flops 4194304 | bytes 6291456 | tf_op jit(solution)/shard_map/convert_element_type | solution.py:286
  108.6 3.3 %collective-permute-start.4 = (bf16[512,512]{1,0:T(8,128)(2,1)}, bf16[512,512]{1,0:T(8,128)(2,1)S(1)}, u32[]{:S(2)}, u32[]{:S(2)}) collective-permute-start(bf16[512,512]{1,0:T(8,128)(2,1)} %get-tuple-element.52), channel_id=1, source_target_pairs={{0,32},{8,40},{16,48},{24,56},{32,0},{40,8},{48,16},{56,24},{64,96... | collective-permute-start | bytes 1572872 | tf_op jit(solution)/shard_map/ppermute | solution.py:257
  113.9 8.4 %all-to-all-done.2 = bf16[8,576,128]{2,1,0:T(8,128)(2,1)S(1)} async-done(((bf16[8,576,128]{2,1,0:T(8,128)(2,1)}), bf16[8,576,128]{2,1,0:T(8,128)(2,1)S(1)}, u32[]{:S(2)}, u32[]{:S(2)}) %all-to-all-start.2) | async-done | bytes 1179680 | tf_op jit(solution)/shard_map/all_to_all | solution.py:289
  122.3 2.9 %reduce_sum.70 = bf16[512,512]{1,0:T(8,128)(2,1)} reduce(bf16[4,512,512]{2,1,0:T(8,128)(2,1)} %all-to-all-done.1, bf16[]{:T(256)} %constant.34.clone.1), dimensions={0}, to_apply=%region_4.5 | reduce | flops 786432 | bytes 2621442 | tf_op jit(solution)/shard_map/reduce_sum | solution.py:305
  125.2 4.8 %all-to-all-start.3 = ((bf16[8,64,512]{2,1,0:T(8,128)(2,1)}), bf16[8,64,512]{2,1,0:T(8,128)(2,1)S(1)}, u32[]{:S(2)}, u32[]{:S(2)}) async-start(bf16[8,64,512]{2,1,0:T(8,128)(2,1)} %bitcast.7), calls=%async_computation.3 | async-start | bytes 1048576 | tf_op jit(solution)/shard_map/all_to_all | solution.py:295
  130.0 5.9 %collective-permute-done.6 = bf16[512,512]{1,0:T(8,128)(2,1)S(1)} collective-permute-done((bf16[512,512]{1,0:T(8,128)(2,1)}, bf16[512,512]{1,0:T(8,128)(2,1)S(1)}, u32[]{:S(2)}, u32[]{:S(2)}) %collective-permute-start.6) | collective-permute-done | bytes 524320 | tf_op jit(solution)/shard_map/ppermute | solution.py:257
  135.9 2.1 %add_convert_fusion.1 = bf16[512,512]{1,0:T(8,128)(2,1)} fusion(bf16[512,512]{1,0:T(8,128)(2,1)S(1)} %copy-done.6, bf16[512,512]{1,0:T(8,128)(2,1)S(1)} %collective-permute-done.6, bf16[512,512]{1,0:T(8,128)(2,1)} %collective-permute-done.5, bf16[512,512]{1,0:T(8,128)(2,1)S(1)} %collective-permute-done.4), kind=kLoop, calls=%fused_computation.7 | loop fusion | flops 2097152 | bytes 2621440 | tf_op jit(solution)/shard_map/convert_element_type | solution.py:294
  138.0 3.0 %all-to-all-done.3 = bf16[8,64,512]{2,1,0:T(8,128)(2,1)S(1)} async-done(((bf16[8,64,512]{2,1,0:T(8,128)(2,1)}), bf16[8,64,512]{2,1,0:T(8,128)(2,1)S(1)}, u32[]{:S(2)}, u32[]{:S(2)}) %all-to-all-start.3) | async-done | bytes 524320 | tf_op jit(solution)/shard_map/all_to_all | solution.py:295
  141.1 3.8 %all-to-all-start.4 = ((bf16[8,64,512]{2,1,0:T(8,128)(2,1)}), bf16[8,64,512]{2,1,0:T(8,128)(2,1)S(1)}, u32[]{:S(2)}, u32[]{:S(2)}) async-start(bf16[8,64,512]{2,1,0:T(8,128)(2,1)} %bitcast.8), calls=%async_computation.4 | async-start | bytes 1048576 | tf_op jit(solution)/shard_map/all_to_all | solution.py:295
  146.7 9.2 %all-to-all-done.4 = bf16[8,64,512]{2,1,0:T(8,128)(2,1)S(1)} async-done(((bf16[8,64,512]{2,1,0:T(8,128)(2,1)}), bf16[8,64,512]{2,1,0:T(8,128)(2,1)S(1)}, u32[]{:S(2)}, u32[]{:S(2)}) %all-to-all-start.4) | async-done | bytes 524320 | tf_op jit(solution)/shard_map/all_to_all | solution.py:295
  157.8 2.5 %collective-permute-done.7 = bf16[64,512]{1,0:T(8,128)(2,1)S(1)} collective-permute-done((bf16[64,512]{1,0:T(8,128)(2,1)S(1)}, bf16[64,512]{1,0:T(8,128)(2,1)S(1)}, u32[]{:S(2)}, u32[]{:S(2)}) %collective-permute-start.7) | collective-permute-done | bytes 65568 | tf_op jit(solution)/shard_map/ppermute | solution.py:309
  (42 shorter events, 11.7 us)
Async XLA Ops:
  0.6 4.2 %collective-permute-start = (bf16[576,128]{1,0:T(8,128)(2,1)}, bf16[576,128]{1,0:T(8,128)(2,1)S(1)}, u32[]{:S(2)}, u32[]{:S(2)}) collective-permute-start(bf16[576,128]{1,0:T(8,128)(2,1)} %bitcast.21), channel_id=1, source_target_pairs={{0,8},{8,16},{16,24},{24,32},{32,40},{40,48},{48,56},{56,64},{64,7... | collective-permute-start | bytes 442376 | tf_op jit(solution)/shard_map/ppermute | solution.py:226
  4.8 10.9 %copy-start.1 = (bf16[128,6144]{1,0:T(8,128)(2,1)S(1)}, bf16[128,6144]{1,0:T(8,128)(2,1)}, u32[]{:S(2)}) copy-start(bf16[128,6144]{1,0:T(8,128)(2,1)} %q_ref.5) | copy-start | bytes 4718596
  4.8 10.9 %copy-start.2 = (bf16[128,4096]{1,0:T(8,128)(2,1)S(1)}, bf16[128,4096]{1,0:T(8,128)(2,1)}, u32[]{:S(2)}) copy-start(bf16[128,4096]{1,0:T(8,128)(2,1)} %g_ref.5) | copy-start | bytes 3145732
  7.1 25.9 %all-to-all-start = ((bf16[8,576,128]{2,1,0:T(8,128)(2,1)}), bf16[8,576,128]{2,1,0:T(8,128)(2,1)}, u32[]{:S(2)}, u32[]{:S(2)}) async-start(bf16[8,576,128]{2,1,0:T(8,128)(2,1)} %broadcast_select_fusion), calls=%async_computation | async-start | bytes 2359296 | tf_op jit(solution)/shard_map/all_to_all | solution.py:242
  15.7 3.4 %copy-start = (bf16[512,8192]{1,0:T(8,128)(2,1)S(1)}, bf16[512,8192]{1,0:T(8,128)(2,1)}, u32[]{:S(2)}) copy-start(bf16[512,8192]{1,0:T(8,128)(2,1)} %w_ref.5) | copy-start | bytes 25165828
  23.5 2.3 %copy-start.3 = (bf16[4096,576]{1,0:T(8,128)(2,1)}, bf16[4096,576]{1,0:T(8,128)(2,1)S(1)}, u32[]{:S(2)}) copy-start(bf16[4096,576]{1,0:T(8,128)(2,1)S(1)} %get-tuple-element.27.qc_ref) | copy-start | bytes 14155780
  25.8 2.0 %copy-start.4 = (bf16[4096,512]{1,0:T(8,128)(2,1)}, bf16[4096,512]{1,0:T(8,128)(2,1)S(1)}, u32[]{:S(2)}) copy-start(bf16[4096,512]{1,0:T(8,128)(2,1)S(1)} %get-tuple-element.28.ga_ref) | copy-start | bytes 12582916
  59.2 4.5 %collective-permute-start.1 = (bf16[2048,512]{1,0:T(8,128)(2,1)}, bf16[2048,512]{1,0:T(8,128)(2,1)}, u32[]{:S(2)}, u32[]{:S(2)}) collective-permute-start(bf16[2048,512]{1,0:T(8,128)(2,1)} %get-tuple-element.30), channel_id=1, source_target_pairs={{0,8},{8,0},{16,24},{24,16},{32,40},{40,32},{48,56},{56,48},{64,72... | collective-permute-start | bytes 6291464 | tf_op jit(solution)/shard_map/ppermute | solution.py:262
  67.9 32.9 %all-to-all-start.1 = ((bf16[4,512,512]{2,1,0:T(8,128)(2,1)}), bf16[4,512,512]{2,1,0:T(8,128)(2,1)}, u32[]{:S(2)}, u32[]{:S(2)}) async-start(bf16[4,512,512]{2,1,0:T(8,128)(2,1)} %bitcast.19), calls=%async_computation.1 | async-start | bytes 4194304 | tf_op jit(solution)/shard_map/all_to_all | solution.py:273
  100.5 4.8 %copy-start.5 = (bf16[2048,512]{1,0:T(8,128)(2,1)S(1)}, bf16[2048,512]{1,0:T(8,128)(2,1)}, u32[]{:S(2)}) copy-start(bf16[2048,512]{1,0:T(8,128)(2,1)} %get-tuple-element.43) | copy-start | bytes 6291460
  100.8 4.5 %collective-permute-start.2 = (bf16[2048,512]{1,0:T(8,128)(2,1)}, bf16[2048,512]{1,0:T(8,128)(2,1)}, u32[]{:S(2)}, u32[]{:S(2)}) collective-permute-start(bf16[2048,512]{1,0:T(8,128)(2,1)} %get-tuple-element.44), channel_id=1, source_target_pairs={{0,8},{8,0},{16,24},{24,16},{32,40},{40,32},{48,56},{56,48},{64,72... | collective-permute-start | bytes 6291464 | tf_op jit(solution)/shard_map/ppermute | solution.py:282
  100.8 21.5 %all-to-all-start.2 = ((bf16[8,576,128]{2,1,0:T(8,128)(2,1)}), bf16[8,576,128]{2,1,0:T(8,128)(2,1)S(1)}, u32[]{:S(2)}, u32[]{:S(2)}) async-start(bf16[8,576,128]{2,1,0:T(8,128)(2,1)} %get-tuple-element.46), calls=%async_computation.2 | async-start | bytes 2359296 | tf_op jit(solution)/shard_map/all_to_all | solution.py:289
  108.6 27.3 %copy-start.6 = (bf16[512,512]{1,0:T(8,128)(2,1)S(1)}, bf16[512,512]{1,0:T(8,128)(2,1)}, u32[]{:S(2)}) copy-start(bf16[512,512]{1,0:T(8,128)(2,1)} %get-tuple-element.49) | copy-start | bytes 1572868
  108.6 21.4 %collective-permute-start.4 = (bf16[512,512]{1,0:T(8,128)(2,1)}, bf16[512,512]{1,0:T(8,128)(2,1)S(1)}, u32[]{:S(2)}, u32[]{:S(2)}) collective-permute-start(bf16[512,512]{1,0:T(8,128)(2,1)} %get-tuple-element.52), channel_id=1, source_target_pairs={{0,32},{8,40},{16,48},{24,56},{32,0},{40,8},{48,16},{56,24},{64,96... | collective-permute-start | bytes 1572872 | tf_op jit(solution)/shard_map/ppermute | solution.py:257
  111.9 24.0 %collective-permute-start.6 = (bf16[512,512]{1,0:T(8,128)(2,1)}, bf16[512,512]{1,0:T(8,128)(2,1)S(1)}, u32[]{:S(2)}, u32[]{:S(2)}) collective-permute-start(bf16[512,512]{1,0:T(8,128)(2,1)} %get-tuple-element.53), channel_id=1, source_target_pairs={{0,48},{8,56},{16,0},{24,8},{32,16},{40,24},{48,32},{56,40},{64,11... | collective-permute-start | bytes 1572872 | tf_op jit(solution)/shard_map/ppermute | solution.py:257
  113.2 22.7 %collective-permute-start.5 = (bf16[512,512]{1,0:T(8,128)(2,1)}, bf16[512,512]{1,0:T(8,128)(2,1)}, u32[]{:S(2)}, u32[]{:S(2)}) collective-permute-start(bf16[512,512]{1,0:T(8,128)(2,1)} %get-tuple-element.54), channel_id=1, source_target_pairs={{0,16},{8,24},{16,32},{24,40},{32,48},{40,56},{48,0},{56,8},{64,80... | collective-permute-start | bytes 1572872 | tf_op jit(solution)/shard_map/ppermute | solution.py:257
  125.2 15.8 %all-to-all-start.3 = ((bf16[8,64,512]{2,1,0:T(8,128)(2,1)}), bf16[8,64,512]{2,1,0:T(8,128)(2,1)S(1)}, u32[]{:S(2)}, u32[]{:S(2)}) async-start(bf16[8,64,512]{2,1,0:T(8,128)(2,1)} %bitcast.7), calls=%async_computation.3 | async-start | bytes 1048576 | tf_op jit(solution)/shard_map/all_to_all | solution.py:295
  141.1 14.9 %all-to-all-start.4 = ((bf16[8,64,512]{2,1,0:T(8,128)(2,1)}), bf16[8,64,512]{2,1,0:T(8,128)(2,1)S(1)}, u32[]{:S(2)}, u32[]{:S(2)}) async-start(bf16[8,64,512]{2,1,0:T(8,128)(2,1)} %bitcast.8), calls=%async_computation.4 | async-start | bytes 1048576 | tf_op jit(solution)/shard_map/all_to_all | solution.py:295
  145.3 11.8 %collective-permute-start.3 = (bf16[576,128]{1,0:T(8,128)(2,1)S(1)}, bf16[576,128]{1,0:T(8,128)(2,1)S(1)}, u32[]{:S(2)}, u32[]{:S(2)}) collective-permute-start(bf16[576,128]{1,0:T(8,128)(2,1)S(1)} %get-tuple-element.50), channel_id=1, source_target_pairs={{8,0},{16,8},{24,16},{32,24},{40,32},{48,40},{56,48},{64,56},{72,6... | collective-permute-start | bytes 442376 | tf_op jit(solution)/shard_map/ppermute | solution.py:226
  156.0 4.3 %collective-permute-start.7 = (bf16[64,512]{1,0:T(8,128)(2,1)S(1)}, bf16[64,512]{1,0:T(8,128)(2,1)S(1)}, u32[]{:S(2)}, u32[]{:S(2)}) collective-permute-start(bf16[64,512]{1,0:T(8,128)(2,1)S(1)} %select_convert_fusion), channel_id=1, source_target_pairs={{0,64},{8,72},{16,80},{24,88},{32,96},{40,104},{48,112},{56,120},{... | collective-permute-start | bytes 196616 | tf_op jit(solution)/shard_map/ppermute | solution.py:309

commit v4 on v3

--- a/solution.py
+++ b/solution.py
@@ -287,7 +287,9 @@
 
     moved = [along_y(piece(by), by) for by in (2, 1, 3)]
     arrived = lax.all_to_all(dkeys, "inner", split_axis=0, concat_axis=0, tiled=True)
-    own_piece, first, arrived = lax.optimization_barrier((piece(0), first, arrived))
+    own_piece, first = lax.optimization_barrier((piece(0), first))
+    first = jnp.sum(first.astype(F32), axis=0).astype(BF16)
+    own_piece, first, arrived = lax.optimization_barrier((own_piece, first, arrived))
     second = sum(m.astype(F32) for m in moved) + own_piece.astype(F32)
 
     def along_inner(part):
@@ -302,7 +304,7 @@
     next_term = shifted(later_term.astype(BF16), "outer", -1).astype(F32)
     grad_compressed = (own_term + next_term).astype(BF16).T
 
-    first = along_inner(jnp.sum(first.astype(F32), axis=0))
+    first = along_inner(first)
     second = along_inner(second)
     low = outer < 8
     crossing = jnp.where(low, second, first).astype(BF16)

time: 162 us -> 162 us (level)
  waiting for transfers between devices: 38.7 us -> 35.8 us
  starting transfers between devices: 36.5 us -> 39.3 us
    all_to_all x2, starting transfers between devices: 8.54 us -> 11.4 us  [along_inner(): lax.all_to_all(part, 'inner', split_axis=0, concat_axis=0, tiled=True)]
    ppermute x3, waiting for transfers between devices: 5.93 us -> 8.8 us  [along_y(): lax.ppermute(shard, 'outer', [(o, o // 8 * 8 + (o % 8 + 2 * by) % 8) for...]
    all_to_all x2, waiting for transfers between devices: 12.2 us -> 9.37 us  [along_inner(): lax.all_to_all(part, 'inner', split_axis=0, concat_axis=0, tiled=True)]
    all_to_all x1, waiting for transfers between devices: 8.43 us -> 5.56 us  [body(): lax.all_to_all(dkeys, 'inner', split_axis=0, concat_axis=0, tiled=True)]
where the time goes in v4:
time: 162 us; the launch traced here: 161 us
  Pallas kernels  57.5 us (35%)
  starting transfers between devices  39.3 us (24%)
  waiting for transfers between devices  35.8 us (22%)
  other arithmetic  19.7 us (12%)
  local copies, waits for them, and re-layouts  7.85 us (5%)
    pallas_call x2, Pallas kernels, attend_chunk(): pl.pallas_call(functools.partial(attend_kernel, scale=scale, is_first=is_...  53.1 us
    all_to_all x2, starting transfers between devices, along_inner(): lax.all_to_all(part, 'inner', split_axis=0, concat_axis=0, tiled=True)  11.4 us
    all_to_all x2, waiting for transfers between devices, along_inner(): lax.all_to_all(part, 'inner', split_axis=0, concat_axis=0, tiled=True)  9.37 us
    ppermute x3, waiting for transfers between devices, along_y(): lax.ppermute(shard, 'outer', [(o, o // 8 * 8 + (o % 8 + 2 * by) % 8) for...  8.8 us
    all_to_all x1, starting transfers between devices, body(): lax.all_to_all(outgoing, 'inner', split_axis=0, concat_axis=0, tiled=True)  8.31 us
    unnamed x14, local copies, waits for them, and re-layouts  7.71 us
    all_to_all x1, starting transfers between devices, body(): lax.all_to_all(pair.reshape(4, 512, LATENT), 'outer', split_axis=0, conca...  5.8 us
    all_to_all x1, waiting for transfers between devices, body(): lax.all_to_all(dkeys, 'inner', split_axis=0, concat_axis=0, tiled=True)  5.56 us
  transfers between devices with their start and end apart: 13, of which 9 were waited for; matrix products, arithmetic and copies ran while one was open for 8% of the time, Pallas kernels for 19%

profile of v4, /device:TPU:0, one launch (start us, length us, event | category | flops | bytes accessed | tf_op | source)
XLA Modules:
  0.0 161.0 jit_solution(3255282728394611059)
XLA Ops:
  0.6 1.3 collective-permute-start
  4.8 2.2 %broadcast_select_fusion = bf16[8,576,128]{2,1,0:T(8,128)(2,1)} fusion(pred[8]{0:T(512)(128)(4,1)S(1)} %iota_compare_fusion.3, bf16[576,128]{1,0:T(8,128)(2,1)S(1)} %collective-permute-done, bf16[576,128]{1,0:T(8,128)(2,1)} %bitcast.22), kind=kLoop, calls=%fused_computation.5 | loop fusion | flops 589824 | bytes 1474568 | tf_op jit(solution)/shard_map/jit(_where)/select_n | solution.py:241
  7.1 8.3 %all-to-all-start = ((bf16[8,576,128]{2,1,0:T(8,128)(2,1)}), bf16[8,576,128]{2,1,0:T(8,128)(2,1)}, u32[]{:S(2)}, u32[]{:S(2)}) async-start(bf16[8,576,128]{2,1,0:T(8,128)(2,1)} %broadcast_select_fusion), calls=%async_computation | async-start | bytes 2359296 | tf_op jit(solution)/shard_map/all_to_all | solution.py:242
  15.7 3.4 %copy-done = bf16[512,8192]{1,0:T(8,128)(2,1)S(1)} copy-done((bf16[512,8192]{1,0:T(8,128)(2,1)S(1)}, bf16[512,8192]{1,0:T(8,128)(2,1)}, u32[]{:S(2)}) %copy-start) | copy-done | bytes 8388632
  19.1 4.4 %absorb.1 = (bf16[4096,576]{1,0:T(8,128)(2,1)S(1)}, bf16[4096,512]{1,0:T(8,128)(2,1)S(1)}) custom-call(bf16[128,6144]{1,0:T(8,128)(2,1)S(1)} %copy-done.1, bf16[128,4096]{1,0:T(8,128)(2,1)S(1)} %copy-done.2, bf16[512,8192]{1,0:T(8,128)(2,1)S(1)} %copy-done), custom_call_target="tpu_custom_call" | custom-call | flops 6000000000 | bytes 20000000 | tf_op jit(solution)/shard_map/absorb/pallas_call | solution.py:55
  23.5 2.3 %copy-done.3 = bf16[4096,576]{1,0:T(8,128)(2,1)} copy-done((bf16[4096,576]{1,0:T(8,128)(2,1)}, bf16[4096,576]{1,0:T(8,128)(2,1)S(1)}, u32[]{:S(2)}) %copy-start.3) | copy-done | bytes 4718616
  25.8 2.0 %copy-done.4 = bf16[4096,512]{1,0:T(8,128)(2,1)} copy-done((bf16[4096,512]{1,0:T(8,128)(2,1)}, bf16[4096,512]{1,0:T(8,128)(2,1)S(1)}, u32[]{:S(2)}) %copy-start.4) | copy-done | bytes 4194328
  27.8 5.1 %all-to-all-done.keys_ref = bf16[8,576,128]{2,1,0:T(8,128)(2,1)} async-done(((bf16[8,576,128]{2,1,0:T(8,128)(2,1)}), bf16[8,576,128]{2,1,0:T(8,128)(2,1)}, u32[]{:S(2)}, u32[]{:S(2)}) %all-to-all-start) | async-done | bytes 1179680 | tf_op jit(solution)/shard_map/all_to_all | solution.py:242
  32.9 26.3 %attend.2 = (bf16[128,4096]{1,0:T(8,128)(2,1)}, bf16[128,6144]{1,0:T(8,128)(2,1)}, bf16[2048,512]{1,0:T(8,128)(2,1)}, bf16[2048,512]{1,0:T(8,128)(2,1)}, f32[576,1024]{1,0:T(8,128)}) custom-call(s32[2]{0:T(128)S(1)} %pad_add_fusion.1.core_ref, bf16[8,576,128]{2,1,0:T(8,128)(2,1)} %all-to-all-done.keys_ref, f32[128,1024]{1,0:T(8,128)S(1)} %fusion.3.bias_ref, ...), custom_call_target="tpu_custom_call" | custom-call | flops 16000000000 | bytes 16000000 | tf_op jit(solution)/shard_map/attend/pallas_call | solution.py:177
  59.7 4.1 %collective-permute-done.1 = bf16[2048,512]{1,0:T(8,128)(2,1)} collective-permute-done((bf16[2048,512]{1,0:T(8,128)(2,1)}, bf16[2048,512]{1,0:T(8,128)(2,1)}, u32[]{:S(2)}, u32[]{:S(2)}) %collective-permute-start.1) | collective-permute-done | bytes 2097184 | tf_op jit(solution)/shard_map/ppermute | solution.py:262
  63.7 4.2 %add_convert_fusion = bf16[2048,512]{1,0:T(8,128)(2,1)} fusion(bf16[2048,512]{1,0:T(8,128)(2,1)} %collective-permute-done.1, bf16[2048,512]{1,0:T(8,128)(2,1)} %get-tuple-element.31), kind=kLoop, calls=%fused_computation | loop fusion | flops 4194304 | bytes 6291456 | tf_op jit(solution)/shard_map/convert_element_type | solution.py:263
  67.9 5.8 %all-to-all-start.1 = ((bf16[4,512,512]{2,1,0:T(8,128)(2,1)}), bf16[4,512,512]{2,1,0:T(8,128)(2,1)}, u32[]{:S(2)}, u32[]{:S(2)}) async-start(bf16[4,512,512]{2,1,0:T(8,128)(2,1)} %bitcast.19), calls=%async_computation.1 | async-start | bytes 4194304 | tf_op jit(solution)/shard_map/all_to_all | solution.py:273
  73.7 26.8 %attend.3 = (bf16[128,4096]{1,0:T(8,128)(2,1)}, bf16[128,6144]{1,0:T(8,128)(2,1)}, bf16[2048,512]{1,0:T(8,128)(2,1)}, bf16[2048,512]{1,0:T(8,128)(2,1)}, bf16[8,576,128]{2,1,0:T(8,128)(2,1)}) custom-call(s32[2]{0:T(128)S(1)} %pad_add_fusion.core_ref, bf16[8,576,128]{2,1,0:T(8,128)(2,1)} %all-to-all-done.keys_ref, ...), custom_call_target="tpu_custom_call", output_to_operand_aliasing={{0}: (9, {}), {1}: (10, {})} | custom-call | flops 16000000000 | bytes 16000000 | tf_op jit(solution)/shard_map/attend/pallas_call | solution.py:177
  100.8 4.4 %all-to-all-start.2 = ((bf16[8,576,128]{2,1,0:T(8,128)(2,1)}), bf16[8,576,128]{2,1,0:T(8,128)(2,1)S(1)}, u32[]{:S(2)}, u32[]{:S(2)}) async-start(bf16[8,576,128]{2,1,0:T(8,128)(2,1)} %get-tuple-element.50), calls=%async_computation.2 | async-start | bytes 2359296 | tf_op jit(solution)/shard_map/all_to_all | solution.py:289
  105.3 3.3 %add_convert_fusion.4 = (bf16[512,512]{1,0:T(8,128)(2,1)}, bf16[512,512]{1,0:T(8,128)(2,1)}, bf16[512,512]{1,0:T(8,128)(2,1)}, bf16[512,512]{1,0:T(8,128)(2,1)}) fusion(bf16[2048,512]{1,0:T(8,128)(2,1)} %collective-permute-done.2, bf16[2048,512]{1,0:T(8,128)(2,1)S(1)} %copy-done.5), kind=kLoop, calls=%fused_computation.10 | loop fusion | flops 4194304 | bytes 6291456 | tf_op jit(solution)/shard_map/convert_element_type | solution.py:286
  108.6 3.3 %collective-permute-start.4 = (bf16[512,512]{1,0:T(8,128)(2,1)}, bf16[512,512]{1,0:T(8,128)(2,1)S(1)}, u32[]{:S(2)}, u32[]{:S(2)}) collective-permute-start(bf16[512,512]{1,0:T(8,128)(2,1)} %get-tuple-element.56), channel_id=1, source_target_pairs={{0,32},{8,40},{16,48},{24,56},{32,0},{40,8},{48,16},{56,24},{64,96... | collective-permute-start | bytes 1572872 | tf_op jit(solution)/shard_map/ppermute | solution.py:257
  113.9 2.9 %reduce_sum.68 = bf16[512,512]{1,0:T(8,128)(2,1)} reduce(bf16[4,512,512]{2,1,0:T(8,128)(2,1)} %all-to-all-done.1, bf16[]{:T(256)} %constant.34.clone.1), dimensions={0}, to_apply=%region_2.3 | reduce | flops 786432 | bytes 2621442 | tf_op jit(solution)/shard_map/reduce_sum | solution.py:291
  116.8 5.6 %all-to-all-done.2 = bf16[8,576,128]{2,1,0:T(8,128)(2,1)S(1)} async-done(((bf16[8,576,128]{2,1,0:T(8,128)(2,1)}), bf16[8,576,128]{2,1,0:T(8,128)(2,1)S(1)}, u32[]{:S(2)}, u32[]{:S(2)}) %all-to-all-start.2) | async-done | bytes 1179680 | tf_op jit(solution)/shard_map/all_to_all | solution.py:289
  122.3 4.8 %all-to-all-start.3 = ((bf16[8,64,512]{2,1,0:T(8,128)(2,1)}), bf16[8,64,512]{2,1,0:T(8,128)(2,1)S(1)}, u32[]{:S(2)}, u32[]{:S(2)}) async-start(bf16[8,64,512]{2,1,0:T(8,128)(2,1)} %bitcast.7), calls=%async_computation.3 | async-start | bytes 1048576 | tf_op jit(solution)/shard_map/all_to_all | solution.py:297
  127.1 8.8 %collective-permute-done.6 = bf16[512,512]{1,0:T(8,128)(2,1)S(1)} collective-permute-done((bf16[512,512]{1,0:T(8,128)(2,1)}, bf16[512,512]{1,0:T(8,128)(2,1)S(1)}, u32[]{:S(2)}, u32[]{:S(2)}) %collective-permute-start.6) | collective-permute-done | bytes 524320 | tf_op jit(solution)/shard_map/ppermute | solution.py:257
  135.9 2.1 %add_convert_fusion.1 = bf16[512,512]{1,0:T(8,128)(2,1)} fusion(bf16[512,512]{1,0:T(8,128)(2,1)S(1)} %copy-done.6, bf16[512,512]{1,0:T(8,128)(2,1)S(1)} %collective-permute-done.6, bf16[512,512]{1,0:T(8,128)(2,1)} %collective-permute-done.5, bf16[512,512]{1,0:T(8,128)(2,1)S(1)} %collective-permute-done.4), kind=kLoop, calls=%fused_computation.7 | loop fusion | flops 2097152 | bytes 2621440 | tf_op jit(solution)/shard_map/convert_element_type | solution.py:296
  138.2 6.6 %all-to-all-start.4 = ((bf16[8,64,512]{2,1,0:T(8,128)(2,1)}), bf16[8,64,512]{2,1,0:T(8,128)(2,1)S(1)}, u32[]{:S(2)}, u32[]{:S(2)}) async-start(bf16[8,64,512]{2,1,0:T(8,128)(2,1)} %bitcast.8), calls=%async_computation.4 | async-start | bytes 1048576 | tf_op jit(solution)/shard_map/all_to_all | solution.py:297
  146.7 9.2 %all-to-all-done.4 = bf16[8,64,512]{2,1,0:T(8,128)(2,1)S(1)} async-done(((bf16[8,64,512]{2,1,0:T(8,128)(2,1)}), bf16[8,64,512]{2,1,0:T(8,128)(2,1)S(1)}, u32[]{:S(2)}, u32[]{:S(2)}) %all-to-all-start.4) | async-done | bytes 524320 | tf_op jit(solution)/shard_map/all_to_all | solution.py:297
  157.8 2.5 %collective-permute-done.7 = bf16[64,512]{1,0:T(8,128)(2,1)S(1)} collective-permute-done((bf16[64,512]{1,0:T(8,128)(2,1)S(1)}, bf16[64,512]{1,0:T(8,128)(2,1)S(1)}, u32[]{:S(2)}, u32[]{:S(2)}) %collective-permute-start.7) | collective-permute-done | bytes 65568 | tf_op jit(solution)/shard_map/ppermute | solution.py:311
  (42 shorter events, 10.6 us)
Async XLA Ops:
  0.6 4.2 %collective-permute-start = (bf16[576,128]{1,0:T(8,128)(2,1)}, bf16[576,128]{1,0:T(8,128)(2,1)S(1)}, u32[]{:S(2)}, u32[]{:S(2)}) collective-permute-start(bf16[576,128]{1,0:T(8,128)(2,1)} %bitcast.21), channel_id=1, source_target_pairs={{0,8},{8,16},{16,24},{24,32},{32,40},{40,48},{48,56},{56,64},{64,7... | collective-permute-start | bytes 442376 | tf_op jit(solution)/shard_map/ppermute | solution.py:226
  4.8 10.9 %copy-start.1 = (bf16[128,6144]{1,0:T(8,128)(2,1)S(1)}, bf16[128,6144]{1,0:T(8,128)(2,1)}, u32[]{:S(2)}) copy-start(bf16[128,6144]{1,0:T(8,128)(2,1)} %q_ref.5) | copy-start | bytes 4718596
  4.8 10.9 %copy-start.2 = (bf16[128,4096]{1,0:T(8,128)(2,1)S(1)}, bf16[128,4096]{1,0:T(8,128)(2,1)}, u32[]{:S(2)}) copy-start(bf16[128,4096]{1,0:T(8,128)(2,1)} %g_ref.5) | copy-start | bytes 3145732
  7.1 25.9 %all-to-all-start = ((bf16[8,576,128]{2,1,0:T(8,128)(2,1)}), bf16[8,576,128]{2,1,0:T(8,128)(2,1)}, u32[]{:S(2)}, u32[]{:S(2)}) async-start(bf16[8,576,128]{2,1,0:T(8,128)(2,1)} %broadcast_select_fusion), calls=%async_computation | async-start | bytes 2359296 | tf_op jit(solution)/shard_map/all_to_all | solution.py:242
  15.7 3.4 %copy-start = (bf16[512,8192]{1,0:T(8,128)(2,1)S(1)}, bf16[512,8192]{1,0:T(8,128)(2,1)}, u32[]{:S(2)}) copy-start(bf16[512,8192]{1,0:T(8,128)(2,1)} %w_ref.5) | copy-start | bytes 25165828
  23.5 2.3 %copy-start.3 = (bf16[4096,576]{1,0:T(8,128)(2,1)}, bf16[4096,576]{1,0:T(8,128)(2,1)S(1)}, u32[]{:S(2)}) copy-start(bf16[4096,576]{1,0:T(8,128)(2,1)S(1)} %get-tuple-element.29.qc_ref) | copy-start | bytes 14155780
  25.8 2.0 %copy-start.4 = (bf16[4096,512]{1,0:T(8,128)(2,1)}, bf16[4096,512]{1,0:T(8,128)(2,1)S(1)}, u32[]{:S(2)}) copy-start(bf16[4096,512]{1,0:T(8,128)(2,1)S(1)} %get-tuple-element.30.ga_ref) | copy-start | bytes 12582916
  59.2 4.5 %collective-permute-start.1 = (bf16[2048,512]{1,0:T(8,128)(2,1)}, bf16[2048,512]{1,0:T(8,128)(2,1)}, u32[]{:S(2)}, u32[]{:S(2)}) collective-permute-start(bf16[2048,512]{1,0:T(8,128)(2,1)} %get-tuple-element.32), channel_id=1, source_target_pairs={{0,8},{8,0},{16,24},{24,16},{32,40},{40,32},{48,56},{56,48},{64,72... | collective-permute-start | bytes 6291464 | tf_op jit(solution)/shard_map/ppermute | solution.py:262
  67.9 32.9 %all-to-all-start.1 = ((bf16[4,512,512]{2,1,0:T(8,128)(2,1)}), bf16[4,512,512]{2,1,0:T(8,128)(2,1)}, u32[]{:S(2)}, u32[]{:S(2)}) async-start(bf16[4,512,512]{2,1,0:T(8,128)(2,1)} %bitcast.19), calls=%async_computation.1 | async-start | bytes 4194304 | tf_op jit(solution)/shard_map/all_to_all | solution.py:273
  100.5 4.8 %copy-start.5 = (bf16[2048,512]{1,0:T(8,128)(2,1)S(1)}, bf16[2048,512]{1,0:T(8,128)(2,1)}, u32[]{:S(2)}) copy-start(bf16[2048,512]{1,0:T(8,128)(2,1)} %get-tuple-element.45) | copy-start | bytes 6291460
  100.8 4.5 %collective-permute-start.2 = (bf16[2048,512]{1,0:T(8,128)(2,1)}, bf16[2048,512]{1,0:T(8,128)(2,1)}, u32[]{:S(2)}, u32[]{:S(2)}) collective-permute-start(bf16[2048,512]{1,0:T(8,128)(2,1)} %get-tuple-element.46), channel_id=1, source_target_pairs={{0,8},{8,0},{16,24},{24,16},{32,40},{40,32},{48,56},{56,48},{64,72... | collective-permute-start | bytes 6291464 | tf_op jit(solution)/shard_map/ppermute | solution.py:282
  100.8 21.5 %all-to-all-start.2 = ((bf16[8,576,128]{2,1,0:T(8,128)(2,1)}), bf16[8,576,128]{2,1,0:T(8,128)(2,1)S(1)}, u32[]{:S(2)}, u32[]{:S(2)}) async-start(bf16[8,576,128]{2,1,0:T(8,128)(2,1)} %get-tuple-element.50), calls=%async_computation.2 | async-start | bytes 2359296 | tf_op jit(solution)/shard_map/all_to_all | solution.py:289
  108.6 27.3 %copy-start.6 = (bf16[512,512]{1,0:T(8,128)(2,1)S(1)}, bf16[512,512]{1,0:T(8,128)(2,1)}, u32[]{:S(2)}) copy-start(bf16[512,512]{1,0:T(8,128)(2,1)} %get-tuple-element.53) | copy-start | bytes 1572868
  108.6 18.5 %collective-permute-start.4 = (bf16[512,512]{1,0:T(8,128)(2,1)}, bf16[512,512]{1,0:T(8,128)(2,1)S(1)}, u32[]{:S(2)}, u32[]{:S(2)}) collective-permute-start(bf16[512,512]{1,0:T(8,128)(2,1)} %get-tuple-element.56), channel_id=1, source_target_pairs={{0,32},{8,40},{16,48},{24,56},{32,0},{40,8},{48,16},{56,24},{64,96... | collective-permute-start | bytes 1572872 | tf_op jit(solution)/shard_map/ppermute | solution.py:257
  111.9 24.0 %collective-permute-start.6 = (bf16[512,512]{1,0:T(8,128)(2,1)}, bf16[512,512]{1,0:T(8,128)(2,1)S(1)}, u32[]{:S(2)}, u32[]{:S(2)}) collective-permute-start(bf16[512,512]{1,0:T(8,128)(2,1)} %get-tuple-element.57), channel_id=1, source_target_pairs={{0,48},{8,56},{16,0},{24,8},{32,16},{40,24},{48,32},{56,40},{64,11... | collective-permute-start | bytes 1572872 | tf_op jit(solution)/shard_map/ppermute | solution.py:257
  113.2 22.7 %collective-permute-start.5 = (bf16[512,512]{1,0:T(8,128)(2,1)}, bf16[512,512]{1,0:T(8,128)(2,1)}, u32[]{:S(2)}, u32[]{:S(2)}) collective-permute-start(bf16[512,512]{1,0:T(8,128)(2,1)} %get-tuple-element.58), channel_id=1, source_target_pairs={{0,16},{8,24},{16,32},{24,40},{32,48},{40,56},{48,0},{56,8},{64,80... | collective-permute-start | bytes 1572872 | tf_op jit(solution)/shard_map/ppermute | solution.py:257
  122.3 15.8 %all-to-all-start.3 = ((bf16[8,64,512]{2,1,0:T(8,128)(2,1)}), bf16[8,64,512]{2,1,0:T(8,128)(2,1)S(1)}, u32[]{:S(2)}, u32[]{:S(2)}) async-start(bf16[8,64,512]{2,1,0:T(8,128)(2,1)} %bitcast.7), calls=%async_computation.3 | async-start | bytes 1048576 | tf_op jit(solution)/shard_map/all_to_all | solution.py:297
  138.2 17.7 %all-to-all-start.4 = ((bf16[8,64,512]{2,1,0:T(8,128)(2,1)}), bf16[8,64,512]{2,1,0:T(8,128)(2,1)S(1)}, u32[]{:S(2)}, u32[]{:S(2)}) async-start(bf16[8,64,512]{2,1,0:T(8,128)(2,1)} %bitcast.8), calls=%async_computation.4 | async-start | bytes 1048576 | tf_op jit(solution)/shard_map/all_to_all | solution.py:297
  145.3 11.8 %collective-permute-start.3 = (bf16[576,128]{1,0:T(8,128)(2,1)S(1)}, bf16[576,128]{1,0:T(8,128)(2,1)S(1)}, u32[]{:S(2)}, u32[]{:S(2)}) collective-permute-start(bf16[576,128]{1,0:T(8,128)(2,1)S(1)} %get-tuple-element.54), channel_id=1, source_target_pairs={{8,0},{16,8},{24,16},{32,24},{40,32},{48,40},{56,48},{64,56},{72,6... | collective-permute-start | bytes 442376 | tf_op jit(solution)/shard_map/ppermute | solution.py:226
  156.0 4.3 %collective-permute-start.7 = (bf16[64,512]{1,0:T(8,128)(2,1)S(1)}, bf16[64,512]{1,0:T(8,128)(2,1)S(1)}, u32[]{:S(2)}, u32[]{:S(2)}) collective-permute-start(bf16[64,512]{1,0:T(8,128)(2,1)S(1)} %select_convert_fusion), channel_id=1, source_target_pairs={{0,64},{8,72},{16,80},{24,88},{32,96},{40,104},{48,112},{56,120},{... | collective-permute-start | bytes 196616 | tf_op jit(solution)/shard_map/ppermute | solution.py:311
